TPU v7x, 256 devices: a whole 4x4x8 slice. The times are simulated.
256 devices in a mesh: section: 8 (over z_lo, core), seg: 32 (over y, z_hi, x).
Axes of the slice: x: 4, y: 4, z: 8 (z_hi: 2, z_lo: 4; z = z_hi * 4 + z_lo), core: 2. Of those that a mesh axis runs over, the one named last changes fastest.
Arguments:
- partition_entry_vectors: bfloat16 [8, 4096, 2048], P('section', 'seg'), may hold values from -6 to 6
- stored_recall_contents: bfloat16 [8, 32, 32, 2048], P('section', 'seg'), may hold values from -6 to 6
- probe_mapping_matrix: bfloat16 [8, 2048, 2048], P('section'), may hold values from -0.125 to 0.125
- entry_rescaling_gain: bfloat16 [8, 2048], P('section'), may hold values from 0.5 to 1.5
- recall_cell_probes: bfloat16 [8, 32, 2048], P('section'), may hold values from -6 to 6
- channel_sharpness: float32 [8, 16], P('section'), may hold values from 4 to 20
- cell_channel_persistence: float32 [8, 32, 32, 16], P('section', 'seg'), may hold values from 0.001 to 1
- piece_genuine_tokens: int32 [32], P('seg'), may hold values from 16 to 128, as said below
- closing_result_slope: bfloat16 [4096, 2048], P('seg'), may hold values from -6 to 6
Outputs:
- hidden_grads: bfloat16 [8, 4096, 2048], P('section', 'seg')
- memory_grads: float32 [8, 32, 32, 2048], P('section', 'seg')
Inputs may be any that keep to these rules, and one draw needn't show every extreme that they name: `piece_genuine_tokens`: the first segment is full.
All inputs are finite; a program needn't handle non-finite values.
Results may differ from a plain program's by a relative error of at most 0.024.
Values may be sent and summed in bfloat16 or wider, within the bound.
No kernel may reach another device: no remote copies, remote signals or barrier semaphores. Data moves between devices by JAX's collectives and lax.ppermute only.
A program may use at most 128 MiB of HBM per device.

v0:
```python
import jax
import jax.numpy as jnp
from jax import lax
from jax.sharding import PartitionSpec as P

HEAD_SIZE = 128


norm_eps = 1e-05
head_eps = 1e-06
highest = lax.Precision.HIGHEST


def prefix(shard, axis, join, neutral):
    count = lax.axis_size(axis)
    place = lax.axis_index(axis)
    ahead = count - 1 - place
    gathered = jax.tree.map(
        lambda a, kind: lax.all_gather(a.astype(kind), axis), shard, (jnp.bfloat16, jnp.bfloat16)
    )
    state = jax.tree.map(lambda a, e: jnp.zeros_like(a) + jnp.asarray(e, a.dtype), shard, neutral)

    def one(hop, state):
        source = count - 1 - hop
        return join(
            state,
            jax.tree.map(
                lambda a, own: lax.dynamic_index_in_dim(a, source, 0, False).astype(own.dtype),
                gathered,
                shard,
            ),
        )

    return lax.fori_loop(0, ahead, one, state)


def passed_along(value, axis, steps):
    count = lax.axis_size(axis)
    initial, last = (max(0, -steps), min(count, count - steps))
    return lax.ppermute(value, axis, [(source, source + steps) for source in range(initial, last)])


def split_heads(matrix):
    return matrix.reshape(matrix.shape[0], -1, HEAD_SIZE)


def inverse_norm(matrix):
    head_parts = split_heads(matrix.astype(jnp.float32))
    return lax.rsqrt(jnp.mean(head_parts * head_parts, axis=-1) + head_eps).T


def normalize_project(tokens_in, gain_row, weight):
    values = tokens_in.astype(jnp.float32)
    row_scale = lax.rsqrt(jnp.mean(values * values, axis=-1, keepdims=True) + norm_eps)
    normed = (values * row_scale * gain_row.astype(jnp.float32)).astype(jnp.bfloat16)
    query_rows = jnp.dot(normed, weight, preferred_element_type=jnp.float32).astype(jnp.bfloat16)
    return (normed, query_rows)


def memory_read(query_rows, memory, smoothing_level):
    query_heads = split_heads(query_rows.astype(jnp.float32))
    memory_heads = split_heads(memory)
    raw_scores = jnp.einsum("rhe,mhe->hrm", query_heads, memory_heads, precision=highest)
    scores = (
        raw_scores
        * (smoothing_level / HEAD_SIZE)[:, None, None]
        * inverse_norm(query_rows)[:, :, None]
        * inverse_norm(memory)[:, None, :]
    )
    weights = jnp.exp(scores)
    weights = (weights / jnp.sum(weights, axis=-1, keepdims=True)).astype(jnp.bfloat16)
    mixed_rows = jnp.einsum(
        "hrm,mhe->rhe", weights.astype(jnp.float32), memory_heads, precision=highest
    )
    return mixed_rows.reshape(query_rows.shape[0], -1)


def memory_write(query_rows, normed, queries_mem, smoothing_level, valid_rows):
    query_heads = split_heads(query_rows.astype(jnp.float32))
    slot_heads = split_heads(queries_mem.astype(jnp.float32))
    value_heads = split_heads(normed.astype(jnp.float32))
    raw_scores = jnp.einsum("mhe,rhe->hmr", slot_heads, query_heads, precision=highest)
    scores = (
        raw_scores
        * (smoothing_level / HEAD_SIZE)[:, None, None]
        * inverse_norm(queries_mem)[:, :, None]
        * inverse_norm(query_rows)[:, None, :]
    )
    weights = jnp.exp(scores) * valid_rows[None, None, :]
    weights = (weights / jnp.sum(weights, axis=-1, keepdims=True)).astype(jnp.bfloat16)
    written = jnp.einsum(
        "hmr,rhe->mhe", weights.astype(jnp.float32), value_heads, precision=highest
    )
    return written.reshape(queries_mem.shape[0], -1)


def combine_heads(earlier, later):
    early_decay, early_sum = earlier
    late_decay, late_sum = later
    slot_count, head_count = late_decay.shape
    scaled = (late_decay[:, :, None] * early_sum.reshape(slot_count, head_count, -1)).reshape(
        early_sum.shape
    )
    return (late_decay * early_decay, scaled + late_sum)


def local(
    partition_entry_vectors,
    stored_recall_contents,
    probe_mapping_matrix,
    entry_rescaling_gain,
    recall_cell_probes,
    channel_sharpness,
    cell_channel_persistence,
    piece_genuine_tokens,
    closing_result_slope,
):
    tokens_here = partition_entry_vectors[0]
    memory_here = stored_recall_contents[0, 0].astype(jnp.float32)
    weight = probe_mapping_matrix[0]
    gain_row = entry_rescaling_gain[0]
    queries_mem = recall_cell_probes[0]
    smoothing_level = channel_sharpness[0]
    decay_rates = cell_channel_persistence[0, 0]
    row_count = tokens_here.shape[0]
    valid_rows = (jnp.arange(row_count) < piece_genuine_tokens[0]).astype(jnp.float32)
    section_pos = lax.axis_index("section")
    sections = lax.axis_size("section")
    (normed, query_rows), pull_front = jax.vjp(
        lambda tokens_held: normalize_project(tokens_held, gain_row, weight), tokens_here
    )
    _, pull_read = jax.vjp(
        lambda query_in, memory_in: memory_read(query_in, memory_in, smoothing_level),
        query_rows,
        memory_here,
    )
    _, pull_write = jax.vjp(
        lambda query_in, normed_in: memory_write(
            query_in, normed_in, queries_mem, smoothing_level, valid_rows
        ),
        query_rows,
        normed,
    )
    widened = jnp.repeat(decay_rates, HEAD_SIZE, axis=1)
    grad_now = (closing_result_slope.astype(jnp.float32) * valid_rows[:, None]).astype(jnp.bfloat16)
    hidden_out = jnp.zeros_like(tokens_here)
    memory_out = jnp.zeros_like(memory_here)
    for turn_index in range(sections):
        active = sections - 1 - turn_index
        is_active = section_pos == active

        def read_back():
            return pull_read(grad_now.astype(jnp.float32))

        def read_skip():
            return (jnp.zeros_like(query_rows), jnp.zeros_like(memory_here))

        query_grad, read_memgrad = lax.cond(is_active, read_back, read_skip)
        swept_rows = prefix(
            (decay_rates, read_memgrad),
            "seg",
            combine_heads,
            (jnp.ones_like(decay_rates), jnp.zeros_like(read_memgrad)),
        )
        memory_grad = swept_rows[1]

        def finish_back():
            grad_query, grad_normed = pull_write((1.0 - widened) * memory_grad)
            (grad_tokens,) = pull_front((grad_normed, query_grad + grad_query))
            return (grad_tokens.astype(jnp.float32) + grad_now.astype(jnp.float32)).astype(
                jnp.bfloat16
            )

        def finish_skip():
            return jnp.zeros_like(tokens_here)

        hidden = lax.cond(is_active, finish_back, finish_skip)
        hidden_out = jnp.where(is_active, hidden, hidden_out)
        memory_out = jnp.where(is_active, memory_grad, memory_out)
        if turn_index + 1 < sections:
            grad_now = passed_along(hidden, "section", -1)
    return (hidden_out[None], memory_out[None, None])


def solution(mesh):
    placed = (
        P("section", "seg", None),
        P("section", "seg", None, None),
        P("section", None, None),
        P("section", None),
        P("section", None, None),
        P("section", None),
        P("section", "seg", None, None),
        P("seg"),
        P("seg", None),
    )
    return jax.shard_map(
        local,
        mesh=mesh,
        in_specs=placed,
        out_specs=(P("section", "seg", None), P("section", "seg", None, None)),
        check_vma=False,
    )
```

profile of v0, /device:TPU:0, one launch (start us, length us, event | category | flops | bytes accessed | tf_op | source)
XLA Modules:
  0.0 1898.1 jit_solution(7249732679108583080)
XLA Ops:
  9.2 4.9 convolution_convert_fusion.48
  21.5 119.9 %all-gather = bf16[32,1,32,16]{2,3,1,0:T(8,128)(2,1)S(1)} all-gather(bf16[1,1,32,16]{2,3,1,0:T(8,128)(2,1)S(1)} %convert_element_type.864), channel_id=2, replica_groups=mesh['section'=8,'seg'=32] {'seg'}, dimensions={0}, use_global_device_ids=true | all-gather | bytes 33792 | tf_op jit(solution)/shard_map/all_gather | solution.py:19
  152.6 81.6 %while.112 = (s32[]{:T(128)}, f32[32,2048]{1,0:T(8,128)}, s32[]{:T(128)}, bf16[32,32,16]{2,1,0:T(8,128)(2,1)}, bf16[32,32,2048]{2,1,0:T(8,128)(2,1)}, /*index=5*/s32[]{:T(128)}, s32[]{:T(128)}, s32[]{:T(128)}, s32[]{:T(128)}) while((s32[]{:T(128)}, f32[32,2048]{1,0:T(8,128)}, s32[]{:T(128)}, bf16[32,32,16]{2,1,0:T(8,128)(2,1)}, ...), condition=%wide.region_10.11_spmd, body=%wide.region_9.10_spmd.sunk | while | flops 197126 | bytes 1184915 | solution.py:34
  236.6 2.8 collective-permute-done
  241.0 141.2 %all-gather.20.cloned.1.call-done = bf16[1024,2048]{1,0:T(8,128)(2,1)} async-done(((bf16[32,2048]{1,0:T(8,128)(2,1)}), bf16[1024,2048]{1,0:T(8,128)(2,1)}) %all-gather.20.cloned.1.call-update) | async-done | bytes 4194320 | tf_op jit(solution)/shard_map/all_gather | solution.py:19
  383.0 82.0 %while.113 = (s32[]{:T(128)}, f32[32,2048]{1,0:T(8,128)}, s32[]{:T(128)}, bf16[32,32,16]{2,1,0:T(8,128)(2,1)}, bf16[32,32,2048]{2,1,0:T(8,128)(2,1)}, /*index=5*/s32[]{:T(128)}, s32[]{:T(128)}, s32[]{:T(128)}, s32[]{:T(128)}) while((s32[]{:T(128)}, f32[32,2048]{1,0:T(8,128)}, s32[]{:T(128)}, bf16[32,32,16]{2,1,0:T(8,128)(2,1)}, ...), condition=%wide.region_24.25_spmd, body=%wide.region_23.24_spmd.sunk | while | flops 197126 | bytes 1184915 | solution.py:34
  467.5 2.8 collective-permute-done.1
  472.1 147.5 %all-gather.22.cloned.1.call-done = bf16[1024,2048]{1,0:T(8,128)(2,1)} async-done(((bf16[32,2048]{1,0:T(8,128)(2,1)}), bf16[1024,2048]{1,0:T(8,128)(2,1)}) %all-gather.22.cloned.1.call-update) | async-done | bytes 4194320 | tf_op jit(solution)/shard_map/all_gather | solution.py:19
  620.3 82.3 %while.114 = (s32[]{:T(128)}, f32[32,2048]{1,0:T(8,128)}, s32[]{:T(128)}, bf16[32,32,16]{2,1,0:T(8,128)(2,1)}, bf16[32,32,2048]{2,1,0:T(8,128)(2,1)}, /*index=5*/s32[]{:T(128)}, s32[]{:T(128)}, s32[]{:T(128)}, s32[]{:T(128)}) while((s32[]{:T(128)}, f32[32,2048]{1,0:T(8,128)}, s32[]{:T(128)}, bf16[32,32,16]{2,1,0:T(8,128)(2,1)}, ...), condition=%wide.region_36.37_spmd, body=%wide.region_35.36_spmd.sunk | while | flops 197126 | bytes 1184915 | solution.py:34
  623.8 1.8 fusion.390
  626.4 1.8 fusion.390
  629.1 1.8 fusion.390
  631.7 1.8 fusion.390
  634.4 1.8 fusion.390
  637.0 1.8 fusion.390
  639.7 1.8 fusion.390
  645.0 1.8 fusion.390
  647.7 1.8 fusion.390
  650.3 1.8 fusion.390
  704.9 2.8 collective-permute-done.2
  709.6 141.3 %all-gather.24.cloned.1.call-done = bf16[1024,2048]{1,0:T(8,128)(2,1)} async-done(((bf16[32,2048]{1,0:T(8,128)(2,1)}), bf16[1024,2048]{1,0:T(8,128)(2,1)}) %all-gather.24.cloned.1.call-update) | async-done | bytes 4194320 | tf_op jit(solution)/shard_map/all_gather | solution.py:19
  851.6 81.8 %while.115 = (s32[]{:T(128)}, f32[32,2048]{1,0:T(8,128)}, s32[]{:T(128)}, bf16[32,32,16]{2,1,0:T(8,128)(2,1)}, bf16[32,32,2048]{2,1,0:T(8,128)(2,1)}, /*index=5*/s32[]{:T(128)}, s32[]{:T(128)}, s32[]{:T(128)}, s32[]{:T(128)}) while((s32[]{:T(128)}, f32[32,2048]{1,0:T(8,128)}, s32[]{:T(128)}, bf16[32,32,16]{2,1,0:T(8,128)(2,1)}, ...), condition=%wide.region_48.49_spmd, body=%wide.region_47.48_spmd.sunk | while | flops 197126 | bytes 1184915 | solution.py:34
  935.9 2.8 collective-permute-done.3
  938.7 2.0 conditional.24
  940.8 148.9 %all-gather.26.cloned.1.call-done = bf16[1024,2048]{1,0:T(8,128)(2,1)} async-done(((bf16[32,2048]{1,0:T(8,128)(2,1)}), bf16[1024,2048]{1,0:T(8,128)(2,1)}) %all-gather.26.cloned.1.call-update) | async-done | bytes 4194320 | tf_op jit(solution)/shard_map/all_gather | solution.py:19
  1090.4 81.5 %while.116 = (s32[]{:T(128)}, f32[32,2048]{1,0:T(8,128)}, s32[]{:T(128)}, bf16[32,32,16]{2,1,0:T(8,128)(2,1)}, bf16[32,32,2048]{2,1,0:T(8,128)(2,1)}, /*index=5*/s32[]{:T(128)}, s32[]{:T(128)}, s32[]{:T(128)}, s32[]{:T(128)}) while((s32[]{:T(128)}, f32[32,2048]{1,0:T(8,128)}, s32[]{:T(128)}, bf16[32,32,16]{2,1,0:T(8,128)(2,1)}, ...), condition=%wide.region_60.61_spmd, body=%wide.region_59.60_spmd.sunk | while | flops 197126 | bytes 1184915 | solution.py:34
  1174.3 2.8 collective-permute-done.4
  1178.9 141.5 %all-gather.28.cloned.1.call-done = bf16[1024,2048]{1,0:T(8,128)(2,1)} async-done(((bf16[32,2048]{1,0:T(8,128)(2,1)}), bf16[1024,2048]{1,0:T(8,128)(2,1)}) %all-gather.28.cloned.1.call-update) | async-done | bytes 4194320 | tf_op jit(solution)/shard_map/all_gather | solution.py:19
  1321.1 81.8 %while.117 = (s32[]{:T(128)}, f32[32,2048]{1,0:T(8,128)}, s32[]{:T(128)}, bf16[32,32,16]{2,1,0:T(8,128)(2,1)}, bf16[32,32,2048]{2,1,0:T(8,128)(2,1)}, /*index=5*/s32[]{:T(128)}, s32[]{:T(128)}, s32[]{:T(128)}, s32[]{:T(128)}) while((s32[]{:T(128)}, f32[32,2048]{1,0:T(8,128)}, s32[]{:T(128)}, bf16[32,32,16]{2,1,0:T(8,128)(2,1)}, ...), condition=%wide.region_72.73_spmd, body=%wide.region_71.72_spmd.sunk | while | flops 197126 | bytes 1184915 | solution.py:34
  1405.3 2.8 collective-permute-done.5
  1410.0 148.7 %all-gather.30.cloned.1.call-done = bf16[1024,2048]{1,0:T(8,128)(2,1)} async-done(((bf16[32,2048]{1,0:T(8,128)(2,1)}), bf16[1024,2048]{1,0:T(8,128)(2,1)}) %all-gather.30.cloned.1.call-update) | async-done | bytes 4194320 | tf_op jit(solution)/shard_map/all_gather | solution.py:19
  1559.4 81.9 %while.118 = (s32[]{:T(128)}, f32[32,2048]{1,0:T(8,128)}, s32[]{:T(128)}, bf16[32,32,16]{2,1,0:T(8,128)(2,1)}, bf16[32,32,2048]{2,1,0:T(8,128)(2,1)}, /*index=5*/s32[]{:T(128)}, s32[]{:T(128)}, s32[]{:T(128)}, s32[]{:T(128)}) while((s32[]{:T(128)}, f32[32,2048]{1,0:T(8,128)}, s32[]{:T(128)}, bf16[32,32,16]{2,1,0:T(8,128)(2,1)}, ...), condition=%wide.region_84.85_spmd, body=%wide.region_83.84_spmd.sunk | while | flops 197126 | bytes 1184915 | solution.py:34
  1644.0 21.6 %collective-permute-done.6 = bf16[128,2048]{1,0:T(8,128)(2,1)} collective-permute-done((bf16[128,2048]{1,0:T(8,128)(2,1)}, bf16[128,2048]{1,0:T(8,128)(2,1)}, u32[]{:S(2)}, u32[]{:S(2)}) %collective-permute-start.6) | collective-permute-done | bytes 524320 | tf_op jit(solution)/shard_map/ppermute | solution.py:40
  1665.6 15.8 conditional.30
  1665.7 2.0 copy.203
  1667.8 2.3 multiply_reduce_fusion.44
  1672.3 2.5 convolution_bitcast_fusion.15
  1674.9 2.1 fusion.256
  1677.7 3.7 fusion.253
  1681.3 102.7 %all-gather.32.cloned.1.call-done = bf16[1024,2048]{1,0:T(8,128)(2,1)} async-done(((bf16[32,2048]{1,0:T(8,128)(2,1)}), bf16[1024,2048]{1,0:T(8,128)(2,1)}) %all-gather.32.cloned.1.call-update) | async-done | bytes 4194320 | tf_op jit(solution)/shard_map/all_gather | solution.py:19
  1784.7 82.2 %while.119 = (s32[]{:T(128)}, f32[32,2048]{1,0:T(8,128)}, s32[]{:T(128)}, bf16[32,32,16]{2,1,0:T(8,128)(2,1)}, bf16[32,32,2048]{2,1,0:T(8,128)(2,1)}, /*index=5*/s32[]{:T(128)}, s32[]{:T(128)}, s32[]{:T(128)}, s32[]{:T(128)}) while((s32[]{:T(128)}, f32[32,2048]{1,0:T(8,128)}, s32[]{:T(128)}, bf16[32,32,16]{2,1,0:T(8,128)(2,1)}, ...), condition=%wide.region_96.97_spmd, body=%wide.region_95.96_spmd.sunk | while | flops 197126 | bytes 1184915 | solution.py:34
  1868.7 20.3 %conditional.31 = (bf16[128,2048]{1,0:T(8,128)(2,1)}) conditional(s32[]{:T(128)} %convert_element_type.863, () %tuple.240, (f32[32,2048]{1,0:T(8,128)}, f32[32,2048]{1,0:T(8,128)}, f32[16,32,128]{2,1,0:T(8,128)}, f32[128,16,128]{2,0,1:T(8,128)S(1)}, f32[16,32,1]{1,0,2:T(8,128)S(1)}, /*index=5*/f32[16,32,1]{1,0,2:T(8,128)S(1)}, ...), branch_computations={%region_97.98_spmd, %region_98.102_spmd} | conditional | flops 1382942848 | bytes 24987748 | solution.py:177
  1868.9 2.9 multiply_reduce_fusion.47
  1873.2 3.1 fusion.273
  1877.4 2.9 convolution_convert_fusion.46
  1880.5 6.4 multiply_reduce_fusion.45
  1886.9 2.1 add_convert_fusion.7
  1889.0 2.0 select_bitcast_fusion
  (874 shorter events, 708.8 us)
Async XLA Ops:
  7.2 144.7 %all-gather.18.cloned.1.call-start = ((), (), s32[]{:S(2)}) async-start(), calls=%async_computation | async-start | bytes 4325376 | tf_op jit(solution)/shard_map/all_gather | solution.py:19
  9.1 5.3 copy-start.21
  9.2 5.4 copy-start.19
  9.2 5.7 copy-start.22
  9.2 10.6 copy-start.18
  14.4 7.1 copy-start.20
  21.4 121.9 %copy-start.17 = (bf16[128,2048]{0,1:T(8,128)(2,1)}, bf16[128,2048]{0,1:T(8,128)(2,1)S(1)}, u32[]{:S(2)}) copy-start(bf16[128,2048]{0,1:T(8,128)(2,1)S(1)} %get-tuple-element.1620) | copy-start | bytes 1572868
  21.5 360.8 %all-gather.20.cloned.1.call-start = ((), (), s32[]{:S(2)}) async-start(), calls=%async_computation.1 | async-start | bytes 4325376 | tf_op jit(solution)/shard_map/all_gather | solution.py:19
  148.4 1.8 copy-start.1
  148.4 85.8 %copy-start.23 = (f32[128,1]{0,1:T(1,128)S(1)}, f32[128,1]{0,1:T(1,128)}, u32[]{:S(2)}) copy-start(f32[128,1]{0,1:T(1,128)} %get-tuple-element.2554) | copy-start | bytes 1540
  235.3 4.1 collective-permute-start
  241.0 378.6 %all-gather.22.cloned.1.call-start = ((), (), s32[]{:S(2)}) async-start(), calls=%async_computation.2 | async-start | bytes 4325376 | tf_op jit(solution)/shard_map/all_gather | solution.py:19
  466.2 4.1 collective-permute-start.1
  472.0 378.9 %all-gather.24.cloned.1.call-start = ((), (), s32[]{:S(2)}) async-start(), calls=%async_computation.3 | async-start | bytes 4325376 | tf_op jit(solution)/shard_map/all_gather | solution.py:19
  703.6 4.1 collective-permute-start.2
  709.6 380.1 %all-gather.26.cloned.1.call-start = ((), (), s32[]{:S(2)}) async-start(), calls=%async_computation.4 | async-start | bytes 4325376 | tf_op jit(solution)/shard_map/all_gather | solution.py:19
  934.6 4.1 collective-permute-start.3
  940.8 379.6 %all-gather.28.cloned.1.call-start = ((), (), s32[]{:S(2)}) async-start(), calls=%async_computation.5 | async-start | bytes 4325376 | tf_op jit(solution)/shard_map/all_gather | solution.py:19
  1173.0 4.1 collective-permute-start.4
  1178.9 379.8 %all-gather.30.cloned.1.call-start = ((), (), s32[]{:S(2)}) async-start(), calls=%async_computation.6 | async-start | bytes 4325376 | tf_op jit(solution)/shard_map/all_gather | solution.py:19
  1404.0 4.1 collective-permute-start.5
  1410.0 374.1 %all-gather.32.cloned.1.call-start = ((), (), s32[]{:S(2)}) async-start(), calls=%async_computation.7 | async-start | bytes 4325376 | tf_op jit(solution)/shard_map/all_gather | solution.py:19
  1642.7 22.9 %collective-permute-start.6 = (bf16[128,2048]{1,0:T(8,128)(2,1)}, bf16[128,2048]{1,0:T(8,128)(2,1)}, u32[]{:S(2)}, u32[]{:S(2)}) collective-permute-start(bf16[128,2048]{1,0:T(8,128)(2,1)} %get-tuple-element.3071), channel_id=1, source_target_pairs={{32,0},{64,32},{96,64},{128,96},{160,128},{192,160},{224,192},{33,... | collective-permute-start | bytes 1572872 | tf_op jit(solution)/shard_map/ppermute | solution.py:40
  1671.6 0.7 copy-start.8
  1681.3 187.4 %copy-start = (f32[16,32,128]{2,1,0:T(8,128)S(1)}, f32[16,32,128]{2,1,0:T(8,128)}, u32[]{:S(2)}) copy-start(f32[16,32,128]{2,1,0:T(8,128)} %get-tuple-element.2544) | copy-start | bytes 786436
  1871.8 1.3 copy-start.16
Sparse Core Ops, SparseCore 0:
  21.6 122.1 all-gather.17
  241.1 141.1 all-gather.19
  472.2 147.3 all-gather.21
  709.7 141.2 all-gather.23
  940.9 148.7 all-gather.25
  1179.0 141.3 all-gather.27
  1410.1 148.5 all-gather.29
  1681.5 102.5 all-gather.31
where the time goes:
time: 1920 us; the launch traced here: 1900 us
  waiting for transfers between devices  1010 us (53%)
  other arithmetic  644 us (34%)
  blocking collectives  120 us (6%)
  local copies, waits for them, and re-layouts  60.9 us (3%)
  matrix products  32.3 us (2%)
    all_gather x8, waiting for transfers between devices, prefix(): lax.all_gather(a.astype(kind), axis)  972 us
    add x248, other arithmetic, combine_heads(): return (late_decay * early_decay, scaled + late_sum)  449 us
    convert_element_type x248, other arithmetic, one(): lax.dynamic_index_in_dim(a, source, 0, False).astype(own.dtype)  173 us
    all_gather x1, blocking collectives, prefix(): lax.all_gather(a.astype(kind), axis)  120 us
    ppermute x7, waiting for transfers between devices, passed_along(): lax.ppermute(value, axis, [(source, source + steps) for source in range(i...  38.6 us
  transfers between devices with their start and end apart: 15, of which 14 were waited for; matrix products, arithmetic and copies ran while one was open for 1% of the time, Pallas kernels for 0%

commit v1 on v0

v1 whole, which is shorter than its diff:
```python
import jax
import jax.numpy as jnp
from jax import lax
from jax.experimental import pallas as pl
from jax.experimental.pallas import tpu as pltpu
from jax.sharding import PartitionSpec as P

D = 2048
HEAD = 128
HEADS = 16
MEM = 32
ROWS = 128
GROUPS = 4
GF = 512
GC = 128
SEGS = 32
ROW = 4
BLOCKS = SEGS // ROW
SECTIONS = 8
AXES = ("section", "seg")

f32 = jnp.float32
bf16 = jnp.bfloat16
norm_eps = 1e-05
head_eps = 1e-06

VMEM = pl.BlockSpec(memory_space=pltpu.VMEM)
SMEM = pl.BlockSpec(memory_space=pltpu.SMEM)
HBM = pl.BlockSpec(memory_space=pl.ANY)


def dot_nn(a, b):
    return lax.dot_general(a, b, (((1,), (0,)), ((), ())), preferred_element_type=f32)


def dot_nt(a, b):
    return lax.dot_general(a, b, (((1,), (1,)), ((), ())), preferred_element_type=f32)


def dot_tn(a, b):
    return lax.dot_general(a, b, (((0,), (0,)), ((), ())), preferred_element_type=f32)


def two_part(value):
    high = value.astype(bf16)
    return high, (value - high.astype(f32)).astype(bf16)


def slot_ones():
    left = lax.broadcasted_iota(jnp.int32, (GC, GC), 0) // MEM
    right = lax.broadcasted_iota(jnp.int32, (GC, GC), 1) // MEM
    return (left == right).astype(f32).astype(bf16)


def sum_slots(value, ones):
    high, low = two_part(value)
    return dot_nn(high, ones) + dot_nn(low, ones)


def spread(parts, rows):
    lane = lax.broadcasted_iota(jnp.int32, (rows, GC), 1) // MEM
    out = jnp.broadcast_to(parts[3], (rows, GC))
    for i in (2, 1, 0):
        out = jnp.where(lane == i, parts[i], out)
    return out


def sharp_row(sharp_ref, g):
    return spread([sharp_ref[0, 4 * g + i] * (1.0 / HEAD) for i in range(4)], 1)


def prepare_kernel(
    x_ref, w_ref, gain_ref, m_ref, p_ref, sharp_ref, count_ref,
    n_ref, qh_ref, invq_ref, rs_ref, bdm_ref, bdmh_ref, bdph_ref, invm_ref, wr_ref, ww_ref,
    bdp_ref,
):
    x = x_ref[...].astype(f32)
    rs = lax.rsqrt(jnp.mean(x * x, axis=-1, keepdims=True) + norm_eps)
    rs_ref[...] = jnp.broadcast_to(rs, (ROWS, HEAD))
    n_ref[...] = (x * rs * gain_ref[...].astype(f32)).astype(bf16)
    for ref in (bdm_ref, bdmh_ref, bdph_ref, bdp_ref):
        ref[...] = jnp.zeros_like(ref)
    ones = slot_ones()
    ones_row = jnp.ones((8, GF), bf16)
    valid = (lax.broadcasted_iota(jnp.int32, (ROWS, GC), 0) < count_ref[0]).astype(f32)
    lane = lax.broadcasted_iota(jnp.int32, (ROWS, HEAD), 1)
    lane_m = lax.broadcasted_iota(jnp.int32, (MEM, HEAD), 1)

    def group(g, carry):
        invq_all, invm_all = carry
        cols = pl.ds(pl.multiple_of(g * GF, GF), GF)
        rows = pl.ds(pl.multiple_of(g * GC, GC), GC)
        qb = dot_nn(n_ref[...], w_ref[:, cols]).astype(bf16)
        invs = []
        for i in range(4):
            at = pl.ds(pl.multiple_of(g * GF + i * HEAD, HEAD), HEAD)
            own = pl.ds(pl.multiple_of(g * GC + i * MEM, MEM), MEM)
            here = pl.ds(i * HEAD, HEAD)
            q = qb[:, i * HEAD : (i + 1) * HEAD].astype(f32)
            inv = lax.rsqrt(jnp.mean(q * q, axis=-1, keepdims=True) + head_eps)
            qh_ref[:, at] = (q * inv).astype(bf16)
            invs.append(inv)
            invq_all = jnp.where(lane == 4 * g + i, inv, invq_all)
            m = m_ref[:, at]
            bdm_ref[own, here] = m
            m = m.astype(f32)
            invm = lax.rsqrt(jnp.mean(m * m, axis=-1, keepdims=True) + head_eps)
            invm_all = jnp.where(lane_m == 4 * g + i, invm, invm_all)
            bdmh_ref[own, here] = (m * invm).astype(bf16)
            p = p_ref[:, at]
            bdp_ref[own, here] = p
            p = p.astype(f32)
            invp = lax.rsqrt(jnp.mean(p * p, axis=-1, keepdims=True) + head_eps)
            bdph_ref[own, here] = (p * invp).astype(bf16)
        invq = spread(invs, ROWS)
        sharp = sharp_row(sharp_ref, g)

        def scores(bd):
            square = bd.astype(f32)
            high, low = two_part(square * square)
            mean = (dot_nt(ones_row, high) + dot_nt(ones_row, low))[0:1] * (1.0 / HEAD)
            return dot_nt(qb, bd) * (sharp * lax.rsqrt(mean + head_eps)) * invq

        read = jnp.exp(scores(bdm_ref[rows, :]))
        wr_ref[:, rows] = (read / sum_slots(read, ones)).astype(bf16)
        write = jnp.exp(scores(bdp_ref[rows, :])) * valid
        ww_ref[:, rows] = (write / jnp.sum(write, axis=0, keepdims=True)).astype(bf16)
        return invq_all, invm_all

    invq_all, invm_all = lax.fori_loop(
        0, GROUPS, group, (jnp.zeros((ROWS, HEAD), f32), jnp.zeros((MEM, HEAD), f32))
    )
    invq_ref[...] = invq_all
    invm_ref[...] = invm_all


def pick_lane(ref, h, rows):
    lane = lax.broadcasted_iota(jnp.int32, (rows, HEAD), 1)
    return jnp.sum(jnp.where(lane == h, ref[...], 0.0), axis=-1, keepdims=True)


def read_kernel(g_ref, wr_ref, bdm_ref, bdmh_ref, qh_ref, invm_ref, sharp_ref, rho_ref, ds_ref):
    ones = slot_ones()

    def group(g, carry):
        cols = pl.ds(pl.multiple_of(g * GF, GF), GF)
        rows = pl.ds(pl.multiple_of(g * GC, GC), GC)
        grad = g_ref[:, cols]
        weights = wr_ref[:, rows]
        wide = weights.astype(f32)
        part = wide * dot_nt(grad, bdm_ref[rows, :])
        ds = ((part - wide * sum_slots(part, ones)) * sharp_row(sharp_ref, g)).astype(bf16)
        ds_ref[:, rows] = ds
        direct = dot_tn(weights, grad)
        scored = dot_tn(ds, qh_ref[:, cols])
        for i in range(4):
            at = pl.ds(pl.multiple_of(g * GF + i * HEAD, HEAD), HEAD)
            own = pl.ds(pl.multiple_of(g * GC + i * MEM, MEM), MEM)
            mh = bdmh_ref[own, i * HEAD : (i + 1) * HEAD].astype(f32)
            a = scored[i * MEM : (i + 1) * MEM, i * HEAD : (i + 1) * HEAD]
            b = direct[i * MEM : (i + 1) * MEM, i * HEAD : (i + 1) * HEAD]
            a = a - mh * (jnp.sum(mh * a, axis=-1, keepdims=True) * (1.0 / HEAD))
            rho_ref[:, at] = (b + pick_lane(invm_ref, 4 * g + i, MEM) * a).astype(bf16)
        return carry

    lax.fori_loop(0, GROUPS, group, 0)


def finish_kernel(
    near_ref, reach_ref, carry_ref, keep_ref, g_ref, n_ref, x_ref, gain_ref, ww_ref, ds_ref,
    bdmh_ref, bdph_ref, qh_ref, invq_ref, rs_ref, sharp_ref, w_hbm,
    hidden_ref, mu_ref,
    w_ref, bdd_ref, dq_ref, dn_ref, sem,
):
    fetch = pltpu.make_async_copy(w_hbm, w_ref, sem)
    fetch.start()
    bdd_ref[...] = jnp.zeros_like(bdd_ref)

    def group(g, carry):
        cols = pl.ds(pl.multiple_of(g * GF, GF), GF)
        rows = pl.ds(pl.multiple_of(g * GC, GC), GC)
        mu = near_ref[:, cols] + reach_ref[:, cols] * carry_ref[:, cols].astype(f32)
        mu_ref[:, cols] = mu
        written = (keep_ref[:, cols] * mu).astype(bf16)
        for i in range(4):
            own = pl.ds(pl.multiple_of(g * GC + i * MEM, MEM), MEM)
            bdd_ref[own, i * HEAD : (i + 1) * HEAD] = written[:, i * HEAD : (i + 1) * HEAD]
        bdd = bdd_ref[rows, :]
        weights = ww_ref[:, rows]
        wide = weights.astype(f32)
        part = wide * dot_nt(n_ref[:, cols], bdd)
        ds = (part - wide * jnp.sum(part, axis=0, keepdims=True)) * sharp_row(sharp_ref, g)
        dn_ref[:, cols] = dot_nn(weights, bdd)
        dqh = dot_nn(ds_ref[:, rows], bdmh_ref[rows, :]) + dot_nn(ds.astype(bf16), bdph_ref[rows, :])
        for i in range(4):
            at = pl.ds(pl.multiple_of(g * GF + i * HEAD, HEAD), HEAD)
            qh = qh_ref[:, at].astype(f32)
            a = dqh[:, i * HEAD : (i + 1) * HEAD]
            a = a - qh * (jnp.sum(qh * a, axis=-1, keepdims=True) * (1.0 / HEAD))
            dq_ref[:, at] = (pick_lane(invq_ref, 4 * g + i, ROWS) * a).astype(bf16)
        return carry

    lax.fori_loop(0, GROUPS, group, 0)
    fetch.wait()
    rs = rs_ref[:, 0:1]

    def project(c, total):
        cols = pl.ds(pl.multiple_of(c * GF, GF), GF)
        dn = dn_ref[:, cols] + dot_nt(dq_ref[...], w_ref[cols, :])
        y = dn * gain_ref[:, cols].astype(f32)
        dn_ref[:, cols] = y
        return total + jnp.sum(y * x_ref[:, cols].astype(f32), axis=-1, keepdims=True)

    total = lax.fori_loop(0, GROUPS, project, jnp.zeros((ROWS, 1), f32))
    shift = total * rs * rs * (1.0 / D)

    def close(c, carry):
        cols = pl.ds(pl.multiple_of(c * GF, GF), GF)
        dx = rs * (dn_ref[:, cols] - x_ref[:, cols].astype(f32) * shift)
        hidden_ref[:, cols] = (g_ref[:, cols].astype(f32) + dx).astype(bf16)
        return carry

    lax.fori_loop(0, GROUPS, close, 0)


def call(kernel, outs, ins, scratch=(), flops=0, moved=0):
    return pl.pallas_call(
        kernel,
        out_shape=[jax.ShapeDtypeStruct(shape, kind) for shape, kind in outs],
        in_specs=ins,
        out_specs=[VMEM] * len(outs),
        scratch_shapes=list(scratch),
        compiler_params=pltpu.CompilerParams(vmem_limit_bytes=44 * 1024 * 1024),
        cost_estimate=pl.CostEstimate(flops=flops, bytes_accessed=moved, transcendentals=0),
    )


def place(section, seg):
    return section * SEGS + seg


def row_swap(value, distance):
    return lax.ppermute(
        value, AXES,
        [(place(s, j), place(s, j ^ distance)) for s in range(SECTIONS) for j in range(SEGS)],
    )


def down_row(b):
    return [
        (place(s, b * ROW + i), place(s, (b - 1) * ROW + i))
        for s in range(SECTIONS)
        for i in range(ROW)
    ]


def widen(value):
    return jnp.repeat(value, HEAD, axis=1)


def local(x, memory, weight, gain, probes, sharp, persistence, counts, slope):
    x, memory, weight, probes = x[0], memory[0, 0], weight[0], probes[0]
    decay = persistence[0, 0]
    section = lax.axis_index("section")
    seg = lax.axis_index("seg")
    spot = seg % ROW
    block = seg // ROW

    n, qh, invq, rs, bdm, bdmh, bdph, invm, wr, ww = call(
        prepare_kernel,
        [
            ((ROWS, D), bf16), ((ROWS, D), bf16), ((ROWS, HEAD), f32), ((ROWS, HEAD), f32),
            ((GF, GF), bf16), ((GF, GF), bf16), ((GF, GF), bf16), ((MEM, HEAD), f32),
            ((ROWS, GF), bf16), ((ROWS, GF), bf16),
        ],
        [VMEM] * 5 + [SMEM] * 2,
        [pltpu.VMEM((GF, GF), bf16)],
        flops=2 * ROWS * D * D, moved=10 << 20,
    )(x, weight, gain, memory, probes, sharp, counts)

    other = row_swap(decay, 1)
    pair = decay * other
    far = row_swap(pair, 2)
    one = jnp.ones_like(decay)
    none = jnp.zeros_like(decay)
    odd, high = spot % 2 == 1, spot >= 2
    own1 = widen(jnp.where(odd, other, one))
    got1 = widen(jnp.where(odd, one, decay))
    own2 = widen(jnp.where(high, far, one))
    got2 = widen(jnp.where(high, one, pair))
    near1 = widen(jnp.where(odd, none, one))
    near2 = widen(jnp.where(high, none, jnp.where(odd, one, other)))
    reach = widen(jnp.where(odd, one, other) * jnp.where(high, one, far))
    whole = widen(pair * far)
    keep = widen(1.0 - decay)

    valid = (jnp.arange(ROWS) < counts[0]).astype(f32)
    start = (slope.astype(f32) * valid[:, None]).astype(bf16)

    def read(grad):
        return call(
            read_kernel,
            [((MEM, D), bf16), ((ROWS, GF), bf16)],
            [VMEM] * 6 + [SMEM],
            flops=2 * ROWS * GF * D, moved=4 << 20,
        )(grad, wr, bdm, bdmh, qh, invm, sharp)

    def finish(near, carry, grad, ds):
        return call(
            finish_kernel,
            [((ROWS, D), bf16), ((MEM, D), f32)],
            [VMEM] * 15 + [SMEM, HBM],
            [
                pltpu.VMEM((D, D), bf16), pltpu.VMEM((GF, GF), bf16), pltpu.VMEM((ROWS, D), bf16),
                pltpu.VMEM((ROWS, D), f32), pltpu.SemaphoreType.DMA,
            ],
            flops=2 * ROWS * D * D, moved=12 << 20,
        )(near, reach, carry, keep, grad, n, x, gain, ww, ds, bdmh, bdph, qh, invq, rs, sharp, weight)

    def turn(grad):
        rho, ds = read(grad)
        get1 = row_swap(rho, 1).astype(f32)
        pair_sum = own1 * rho.astype(f32) + got1 * get1
        get2 = row_swap(pair_sum.astype(bf16), 2).astype(f32)
        row_sum = own2 * pair_sum + got2 * get2
        near = near1 * get1 + near2 * get2
        carry = jnp.zeros((MEM, D), bf16)
        for b in range(BLOCKS - 1, 0, -1):
            def step(carry, b=b):
                moving = (row_sum + whole * carry.astype(f32)).astype(bf16)
                return carry + lax.ppermute(moving, AXES, down_row(b))

            carry = lax.cond((block == b) | (block == b - 1), step, lambda c: c, carry)
        return finish(near, carry, grad, ds)

    state = (start, jnp.zeros((MEM, D), f32))
    grad = start
    for active in range(SECTIONS - 1, -1, -1):
        state = lax.cond(section == active, lambda s, g: turn(g), lambda s, g: s, state, grad)
        if active:
            grad = lax.ppermute(
                state[0], AXES, [(place(active, j), place(active - 1, j)) for j in range(SEGS)]
            )
    return state[0][None], state[1][None, None]


def solution(mesh):
    placed = (
        P("section", "seg", None),
        P("section", "seg", None, None),
        P("section", None, None),
        P("section", None),
        P("section", None, None),
        P("section", None),
        P("section", "seg", None, None),
        P("seg"),
        P("seg", None),
    )
    return jax.shard_map(
        local,
        mesh=mesh,
        in_specs=placed,
        out_specs=(P("section", "seg", None), P("section", "seg", None, None)),
        check_vma=False,
    )
```

time: 1920 us -> 518 us (0.27)
  other arithmetic: 644 us -> 7.51 us
  waiting for transfers between devices: 1010 us -> 446 us
  blocking collectives: 120 us -> 0 us
  local copies, waits for them, and re-layouts: 60.9 us -> 9.12 us
  matrix products: 32.3 us -> 0 us
  Pallas kernels: 0 us -> 22.4 us
    all_gather x8 -> x0, waiting for transfers between devices: 972 us -> none  [prefix(): lax.all_gather(a.astype(kind), axis)]
    add x249 -> x2, other arithmetic: 450 us -> 3.72 us  [the longest x1 2.13 us: turn(): row_sum = own2 * pair_sum + got2 * get2]
    ppermute x7 -> x12, waiting for transfers between devices: 38.6 us -> 446 us  [the longest x7 418 us: local(): lax.ppermute(state[0], AXES, [(place(active, j), place(active - 1, j)) fo...]
    convert_element_type x259 -> x4, other arithmetic: 183 us -> 3.77 us  [the longest x1 2.05 us: local(): start = (slope.astype(f32) * valid[:, None]).astype(bf16)]
    all_gather x1 -> x0, blocking collectives: 120 us -> none  [prefix(): lax.all_gather(a.astype(kind), axis)]
    dot_general x11 -> x0, matrix products: 32.3 us -> none  [the longest x2 11.3 us: normalize_project(): jnp.dot(normed, weight, preferred_element_type=jnp.float32)]
    mul x248 -> x2, local copies, waits for them, and re-layouts: 31 us -> 0.15 us  [the longest x1 0.08 us: local(): reach = widen(jnp.where(odd, one, other) * jnp.where(high, one, far))]
    another operation x33 -> x2, local copies, waits for them, and re-layouts: 23.9 us -> 1.38 us
  transfers between devices with their start and end apart: 15 -> 12, of which waited for: 14 -> 5; matrix products, arithmetic and copies ran while one was open for 1% -> 1% of each run, Pallas kernels for 0% -> 2%
where the time goes in v1:
time: 518 us; the launch traced here: 512 us
  waiting for transfers between devices  446 us (86%)
  Pallas kernels  22.4 us (4%)
  starting transfers between devices  17.3 us (3%)
  local copies, waits for them, and re-layouts  9.12 us (2%)
  loops' own time  8.8 us (2%)
  other arithmetic  7.51 us (1%)
    ppermute x7, waiting for transfers between devices, local(): lax.ppermute(state[0], AXES, [(place(active, j), place(active - 1, j)) fo...  418 us
    ppermute x1, waiting for transfers between devices, step(): return carry + lax.ppermute(moving, AXES, down_row(b))  17.1 us
  transfers between devices with their start and end apart: 12, of which 5 were waited for; matrix products, arithmetic and copies ran while one was open for 1% of the time, Pallas kernels for 2%

profile of v1, /device:TPU:0, one launch (start us, length us, event | category | flops | bytes accessed | tf_op | source)
XLA Modules:
  0.0 512.4 jit_solution(14542666375456111802)
XLA Ops:
  1.4 2.0 multiply_convert_fusion
  3.5 0.9 copy-done
  4.4 0.9 copy-done.1
  5.3 8.7 %shard_map.104 = (bf16[128,2048]{1,0:T(8,128)(2,1)}, bf16[128,2048]{1,0:T(8,128)(2,1)S(1)}, f32[128,128]{1,0:T(8,128)}, f32[128,128]{1,0:T(8,128)}, bf16[512,512...) custom-call(bf16[128,2048]{1,0:T(8,128)(2,1)} %bitcast.50, ...), custom_call_target="tpu_custom_call" | custom-call | flops 1073741824 | bytes 10485760 | tf_op jit(solution)/shard_map/pallas_call | solution.py:269
  14.1 2.6 collective-permute-start.73
  16.8 0.1 broadcast_in_dim.43
  16.9 0.1 broadcast_in_dim.44
  17.0 0.2 copy_bitcast_fusion.6
  17.4 1.9 collective-permute-done.73
  19.5 0.1 broadcast_in_dim.50
  19.7 0.1 broadcast_in_dim.51
  19.8 0.9 copy_bitcast_fusion
  20.7 0.1 broadcast_in_dim.49
  20.9 0.1 broadcast_in_dim.48
  21.0 0.9 copy_bitcast_fusion.2
  21.9 0.1 broadcast_in_dim.47
  22.0 0.1 broadcast_in_dim.46
  22.1 1.0 copy_bitcast_fusion.4
  23.1 0.7 reshape.36
  23.8 0.7 conditional.64
  23.8 0.7 broadcast.49
  24.5 1.4 collective-permute-start.74
  26.0 0.2 conditional.65
  26.2 1.5 collective-permute-start.75
  27.7 1.4 collective-permute-start.76
  29.2 1.4 collective-permute-start.77
  30.6 8.5 %conditional.68 = ((bf16[128,2048]{1,0:T(8,128)(2,1)}, f32[32,2048]{1,0:T(8,128)})) conditional(s32[]{:T(128)} %convert_element_type.619, (bf16[128,2048]{1,0:T(8,128)(2,1)}, f32[32,2048]{1,0:T(8,128)}) %get-tuple-element.1523, (bf16[128,2048]{1,0:T(8,128)(2,1)}, bf16[128,512]{1,0:T(8,128)(2,1)}, bf16[512,512]{1,0:T(8,128)(2,1)}, ...), branch_computations={%region_64.65_spmd, %region_65.80_spmd} | conditional | flops 1345519616 | bytes 35783452 | solution.py:339
  39.1 1.5 collective-permute-start.78
  40.6 1.4 collective-permute-start.79
  42.0 1.3 collective-permute-start.80
  43.3 418.3 %collective-permute-done.80 = bf16[128,2048]{1,0:T(8,128)(2,1)} collective-permute-done((bf16[128,2048]{1,0:T(8,128)(2,1)}, bf16[128,2048]{1,0:T(8,128)(2,1)}, u32[]{:S(2)}, u32[]{:S(2)}) %collective-permute-start.80) | collective-permute-done | bytes 524320 | tf_op jit(solution)/shard_map/ppermute | solution.py:341
  461.6 50.6 %conditional.71 = (bf16[1,128,2048]{2,1,0:T(8,128)(2,1)}, f32[1,1,32,2048]{3,2,1,0:T(8,128)}) conditional(s32[]{:T(128)} %convert_element_type.616, (bf16[128,2048]{1,0:T(8,128)(2,1)}, f32[32,2048]{1,0:T(8,128)}) %get-tuple-element.1526, (bf16[128,2048]{1,0:T(8,128)(2,1)}, bf16[128,512]{1,0:T(8,128)(2,1)}, bf16[512,512]{1,0:T(8,128)(2,1)}, ...), branch_computations={%region_112.113_spmd, %region_113.128_spmd} | conditional | flops 1345519616 | bytes 35800156 | solution.py:339
  461.6 3.9 branch_1_fun.30
  465.5 0.6 collective-permute-start.70
  466.2 4.4 collective-permute-done.70
  470.6 0.7 fusion.31
  471.3 2.7 collective-permute-start.71
  474.0 4.0 collective-permute-done.71
  478.0 0.6 copy-done.29
  478.6 2.1 fusion.30
  480.7 0.7 conditional.49
  480.7 0.7 broadcast.64
  481.4 21.0 %conditional.55 = (bf16[32,2048]{1,0:T(8,128)(2,1)}) conditional(s32[]{:T(128)} %convert_element_type.598, bf16[32,2048]{1,0:T(8,128)(2,1)} %get-tuple-element.1518, (bf16[32,2048]{1,0:T(8,128)(2,1)}, f32[32,2048]{1,0:T(8,128)S(1)}, f32[32,2048]{1,0:T(8,128)}) %tuple.380), branch_computations={%region_126.126_spmd, %region_127.127_spmd} | conditional | flops 327680 | bytes 1703984 | solution.py:333
  481.4 1.0 add_convert_fusion.55
  482.4 1.3 collective-permute-start.69
  483.7 17.1 %collective-permute-done.69 = bf16[32,2048]{1,0:T(8,128)(2,1)S(1)} collective-permute-done((bf16[32,2048]{1,0:T(8,128)(2,1)S(1)}, bf16[32,2048]{1,0:T(8,128)(2,1)S(1)}, u32[]{:S(2)}, u32[]{:S(2)}) %collective-permute-start.69) | collective-permute-done | bytes 131104 | tf_op jit(solution)/shard_map/cond/branch_1_fun/cond/branch_1_fun/ppermute | solution.py:331
  500.8 1.6 add.386
  502.4 9.7 %branch_1_fun.31 = (bf16[128,2048]{1,0:T(8,128)(2,1)}, f32[32,2048]{1,0:T(8,128)}) custom-call(f32[32,2048]{1,0:T(8,128)S(1)} %get-tuple-element.1412.near_ref, f32[32,2048]{1,0:T(8,128)} %get-tuple-element.1334.reach_ref, bf16[32,2048]{1,0:T(8,128)(2,1)} %get-tuple-element.1519.carry_ref, f32[32,2048]{1,0:T(8,128)} %get-tuple-element.1339.keep_ref, ...), custom_call_target="tpu_custom_call" | custom-call | flops 1073741824 | bytes 12582912 | tf_op jit(solution)/shard_map/cond/branch_1_fun/pallas_call | solution.py:309
  (45 shorter events, 0.8 us)
Async XLA Ops:
  0.6 13.4 %copy-start.30 = (f32[1,1,32,16]{2,3,1,0:T(8,128)S(1)}, f32[1,1,32,16]{2,3,1,0:T(8,128)}, u32[]{:S(2)}) copy-start(f32[1,1,32,16]{2,3,1,0:T(8,128)} %param.143) | copy-start | bytes 6148
  0.6 13.4 %collective-permute-start.72 = (f32[32,16]{0,1:T(8,128)}, f32[32,16]{0,1:T(8,128)S(1)}, u32[]{:S(2)}, u32[]{:S(2)}) collective-permute-start(f32[32,16]{0,1:T(8,128)} %bitcast.67), channel_id=1, source_target_pairs={{0,1},{1,0},{2,3},{3,2},{4,5},{5,4},{6,7},{7,6},{8,9},{9,8},{10,11... | collective-permute-start | bytes 6152 | tf_op jit(solution)/shard_map/ppermute | solution.py:243
  1.4 22.4 %copy-start.2 = (bf16[1,128,2048]{2,1,0:T(8,128)(2,1)S(1)}, bf16[1,128,2048]{2,1,0:T(8,128)(2,1)}, u32[]{:S(2)}) copy-start(bf16[1,128,2048]{2,1,0:T(8,128)(2,1)} %param.137) | copy-start | bytes 1572868
  3.5 20.4 %copy-start.19 = (f32[1,16]{1,0:T(1,128)S(1)}, f32[1,16]{1,0:T(1,128)}, u32[]{:S(2)}) copy-start(f32[1,16]{1,0:T(1,128)} %sharp_ref.1) | copy-start | bytes 196
  3.5 0.9 copy-start
  4.4 0.9 copy-start.1
  14.1 5.2 %collective-permute-start.73 = (f32[32,16]{0,1:T(8,128)S(1)}, f32[32,16]{0,1:T(8,128)S(1)}, u32[]{:S(2)}, u32[]{:S(2)}) collective-permute-start(f32[32,16]{0,1:T(8,128)S(1)} %get-tuple-element.1416), channel_id=1, source_target_pairs={{0,2},{1,3},{2,0},{3,1},{4,6},{5,7},{6,4},{7,5},{8,10},{9,11},{10,... | collective-permute-start | bytes 6152 | tf_op jit(solution)/shard_map/ppermute | solution.py:243
  24.5 1.4 collective-permute-start.74
  26.2 1.5 collective-permute-start.75
  27.7 1.5 collective-permute-start.76
  29.2 1.5 collective-permute-start.77
  39.1 1.5 collective-permute-start.78
  40.6 1.5 collective-permute-start.79
  42.0 419.6 %collective-permute-start.80 = (bf16[128,2048]{1,0:T(8,128)(2,1)}, bf16[128,2048]{1,0:T(8,128)(2,1)}, u32[]{:S(2)}, u32[]{:S(2)}) collective-permute-start(bf16[128,2048]{1,0:T(8,128)(2,1)} %get-tuple-element.1462), channel_id=1, source_target_pairs={{32,0},{33,1},{34,2},{35,3},{36,4},{37,5},{38,6},{39,7},{40,8},{41... | collective-permute-start | bytes 1572872 | tf_op jit(solution)/shard_map/ppermute | solution.py:341
  461.6 40.8 %copy-start.9 = (bf16[128,2048]{1,0:T(8,128)(2,1)S(1)}, bf16[128,2048]{1,0:T(8,128)(2,1)}, u32[]{:S(2)}) copy-start(bf16[128,2048]{1,0:T(8,128)(2,1)} %get-tuple-element.1340.n_ref) | copy-start | bytes 1572868 | tf_op jit(solution)/shard_map/cond
  465.5 36.9 %copy-start.10 = (bf16[1,2048]{1,0:T(2,128)(2,1)S(1)}, bf16[1,2048]{1,0:T(2,128)(2,1)}, u32[]{:S(2)}) copy-start(bf16[1,2048]{1,0:T(2,128)(2,1)} %get-tuple-element.1342.gain_ref) | copy-start | bytes 12292 | tf_op jit(solution)/shard_map/cond
  465.5 36.9 %copy-start.21 = (f32[1,16]{1,0:T(1,128)S(1)}, f32[1,16]{1,0:T(1,128)}, u32[]{:S(2)}) copy-start(f32[1,16]{1,0:T(1,128)} %get-tuple-element.1329.sharp_ref) | copy-start | bytes 196 | tf_op jit(solution)/shard_map/cond
  465.5 5.1 collective-permute-start.70
  470.6 7.4 %copy-start.18 = (bf16[32,2048]{1,0:T(8,128)(2,1)}, bf16[32,2048]{1,0:T(8,128)(2,1)S(1)}, u32[]{:S(2)}) copy-start(bf16[32,2048]{1,0:T(8,128)(2,1)S(1)} %collective-permute-done.70) | copy-start | bytes 393220 | tf_op jit(solution)/shard_map/cond
  471.3 6.7 %collective-permute-start.71 = (bf16[32,2048]{1,0:T(8,128)(2,1)}, bf16[32,2048]{1,0:T(8,128)(2,1)S(1)}, u32[]{:S(2)}, u32[]{:S(2)}) collective-permute-start(bf16[32,2048]{1,0:T(8,128)(2,1)} %fusion.31), channel_id=1, source_target_pairs={{0,2},{1,3},{2,0},{3,1},{4,6},{5,7},{6,4},{7,5},{8,10},{9,11},{10,... | collective-permute-start | bytes 393224 | tf_op jit(solution)/shard_map/cond/branch_1_fun/ppermute | solution.py:243
  478.0 0.6 copy-start.29
  482.4 18.4 %collective-permute-start.69 = (bf16[32,2048]{1,0:T(8,128)(2,1)S(1)}, bf16[32,2048]{1,0:T(8,128)(2,1)S(1)}, u32[]{:S(2)}, u32[]{:S(2)}) collective-permute-start(bf16[32,2048]{1,0:T(8,128)(2,1)S(1)} %add_convert_fusion.55), channel_id=1, source_target_pairs={{4,0},{5,1},{6,2},{7,3},{36,32},{37,33},{38,34},{39,35},{68,64},{6... | collective-permute-start | bytes 393224 | tf_op jit(solution)/shard_map/cond/branch_1_fun/cond/branch_1_fun/ppermute | solution.py:331

commit v2 on v1

v2 whole, which is shorter than its diff:
```python
import functools

import jax
import jax.numpy as jnp
from jax import lax
from jax.experimental import pallas as pl
from jax.experimental.pallas import tpu as pltpu
from jax.sharding import PartitionSpec as P

D = 2048
HEAD = 128
HEADS = 16
MEM = 32
ROWS = 128
GROUPS = 4
GF = 512
GC = 128
SEGS = 32
PAIRS = SEGS // 2
SECTIONS = 8
AXES = ("section", "seg")
OWN, GOT, NEAR, REACH, WHOLE, KEEP, SHARP = (k * HEADS for k in range(7))

f32 = jnp.float32
bf16 = jnp.bfloat16
norm_eps = 1e-05
head_eps = 1e-06

VMEM = pl.BlockSpec(memory_space=pltpu.VMEM)
SMEM = pl.BlockSpec(memory_space=pltpu.SMEM)
HBM = pl.BlockSpec(memory_space=pltpu.HBM)
ANY = pl.BlockSpec(memory_space=pl.ANY)


def dot_nn(a, b):
    return lax.dot_general(a, b, (((1,), (0,)), ((), ())), preferred_element_type=f32)


def dot_nt(a, b):
    return lax.dot_general(a, b, (((1,), (1,)), ((), ())), preferred_element_type=f32)


def dot_tn(a, b):
    return lax.dot_general(a, b, (((0,), (0,)), ((), ())), preferred_element_type=f32)


def two_part(value):
    high = value.astype(bf16)
    return high, (value - high.astype(f32)).astype(bf16)


def slot_ones():
    left = lax.broadcasted_iota(jnp.int32, (GC, GC), 0) // MEM
    right = lax.broadcasted_iota(jnp.int32, (GC, GC), 1) // MEM
    return (left == right).astype(f32).astype(bf16)


def sum_slots(value, ones):
    high, low = two_part(value)
    return dot_nn(high, ones) + dot_nn(low, ones)


def spread(parts, rows):
    lane = lax.broadcasted_iota(jnp.int32, (rows, GC), 1) // MEM
    out = jnp.broadcast_to(parts[3], (rows, GC))
    for i in (2, 1, 0):
        out = jnp.where(lane == i, parts[i], out)
    return out


def sharp_row(coef_ref, g):
    at = SHARP + 4 * g
    return spread([coef_ref[0:1, at + i : at + i + 1] for i in range(4)], 1)


def prepare_kernel(
    x_ref, w_hbm, gain_ref, m_ref, p_ref, slope_ref, sharp_ref, count_ref,
    n_ref, qh_ref, invq_ref, rs_ref, bdm_ref, bdmh_ref, bdph_ref, invm_ref, wr_ref, ww_ref, start_ref,
    bdp_ref, w_ref, sem,
):
    fetch = pltpu.make_async_copy(w_hbm, w_ref, sem)
    fetch.start()
    x = x_ref[...].astype(f32)
    rs = lax.rsqrt(jnp.mean(x * x, axis=-1, keepdims=True) + norm_eps)
    rs_ref[...] = jnp.broadcast_to(rs, (ROWS, HEAD))
    n_ref[...] = (x * rs * gain_ref[...].astype(f32)).astype(bf16)
    for ref in (bdm_ref, bdmh_ref, bdph_ref, bdp_ref):
        ref[...] = jnp.zeros_like(ref)
    ones = slot_ones()
    ones_row = jnp.ones((8, GF), bf16)
    valid = (lax.broadcasted_iota(jnp.int32, (ROWS, GC), 0) < count_ref[0]).astype(f32)
    whole = lax.broadcasted_iota(jnp.int32, (ROWS, D), 0) < count_ref[0]
    start_ref[...] = jnp.where(whole, slope_ref[...].astype(f32), 0.0).astype(bf16)
    fetch.wait()
    lane = lax.broadcasted_iota(jnp.int32, (ROWS, HEAD), 1)
    lane_m = lax.broadcasted_iota(jnp.int32, (MEM, HEAD), 1)

    def group(g, carry):
        invq_all, invm_all = carry
        cols = pl.ds(g * GF, GF)
        rows = pl.ds(g * GC, GC)
        qb = dot_nn(n_ref[...], w_ref[:, cols]).astype(bf16)
        invs = []
        for i in range(4):
            at = pl.ds(g * GF + i * HEAD, HEAD)
            own = pl.ds(g * GC + i * MEM, MEM)
            here = pl.ds(i * HEAD, HEAD)
            q = qb[:, i * HEAD : (i + 1) * HEAD].astype(f32)
            inv = lax.rsqrt(jnp.mean(q * q, axis=-1, keepdims=True) + head_eps)
            qh_ref[:, at] = (q * inv).astype(bf16)
            invs.append(inv)
            invq_all = jnp.where(lane == 4 * g + i, inv, invq_all)
            m = m_ref[:, at]
            bdm_ref[own, here] = m
            m = m.astype(f32)
            invm = lax.rsqrt(jnp.mean(m * m, axis=-1, keepdims=True) + head_eps)
            invm_all = jnp.where(lane_m == 4 * g + i, invm, invm_all)
            bdmh_ref[own, here] = (m * invm).astype(bf16)
            p = p_ref[:, at]
            bdp_ref[own, here] = p
            p = p.astype(f32)
            invp = lax.rsqrt(jnp.mean(p * p, axis=-1, keepdims=True) + head_eps)
            bdph_ref[own, here] = (p * invp).astype(bf16)
        invq = spread(invs, ROWS)
        sharp = spread([sharp_ref[0, 4 * g + i] * (1.0 / HEAD) for i in range(4)], 1)

        def scores(bd):
            square = bd.astype(f32)
            high, low = two_part(square * square)
            mean = (dot_nt(ones_row, high) + dot_nt(ones_row, low))[0:1] * (1.0 / HEAD)
            return dot_nt(qb, bd) * (sharp * lax.rsqrt(mean + head_eps)) * invq

        read = jnp.exp(scores(bdm_ref[rows, :]))
        wr_ref[:, rows] = (read / sum_slots(read, ones)).astype(bf16)
        write = jnp.exp(scores(bdp_ref[rows, :])) * valid
        ww_ref[:, rows] = (write / jnp.sum(write, axis=0, keepdims=True)).astype(bf16)
        return invq_all, invm_all

    invq_all, invm_all = jnp.zeros((ROWS, HEAD), f32), jnp.zeros((MEM, HEAD), f32)
    for g in range(GROUPS):
        invq_all, invm_all = group(g, (invq_all, invm_all))
    invq_ref[...] = invq_all
    invm_ref[...] = invm_all


def blank_kernel(*refs):
    pass


def join_kernel(has_carry, step_ref, sum_any, near_any, coef_any, *refs):
    carry_any = refs[0] if has_carry else None
    moving_hbm, mu_hbm, sum_ref, near_ref, carry_ref, coef_ref, moving_ref, mu_ref, sems = refs[-9:]

    @pl.when(step_ref[0] == 0)
    def _():
        sources = [(coef_any, coef_ref), (sum_any, sum_ref), (near_any, near_ref)]
        if has_carry:
            sources.append((carry_any, carry_ref))
        fetch = [pltpu.make_async_copy(*pair, sems.at[k]) for k, pair in enumerate(sources)]
        leave_moving = pltpu.make_async_copy(moving_ref, moving_hbm, sems.at[4])
        leave_mu = pltpu.make_async_copy(mu_ref, mu_hbm, sems.at[5])
        for copy in fetch:
            copy.start()
        for copy in fetch:
            copy.wait()
        near = coef_ref[:, NEAR : NEAR + 1]
        for h in range(HEADS):
            at = pl.ds(h * HEAD, HEAD)
            moving = sum_ref[:, at]
            mu = near * near_ref[:, at].astype(f32)
            if has_carry:
                carry = carry_ref[:, at].astype(f32)
                reach, whole = (coef_ref[:, c + h : c + h + 1] for c in (REACH, WHOLE))
                moving = (moving.astype(f32) + whole * carry).astype(bf16)
                mu = mu + reach * carry
            moving_ref[:, at] = moving
            mu_ref[:, at] = mu
        leave_moving.start()
        leave_mu.start()
        leave_moving.wait()
        leave_mu.wait()


def combine_kernel(rho_ref, get_ref, coef_ref, out_ref):
    for h in range(HEADS):
        at = pl.ds(h * HEAD, HEAD)
        own = coef_ref[:, OWN + h : OWN + h + 1]
        got = coef_ref[:, GOT + h : GOT + h + 1]
        out_ref[:, at] = (own * rho_ref[:, at].astype(f32) + got * get_ref[:, at].astype(f32)).astype(bf16)


def read_kernel(g_ref, wr_ref, bdm_ref, bdmh_ref, qh_ref, invm_ref, coef_ref, rho_ref, ds_ref):
    ones = slot_ones()

    def group(g, carry):
        cols = pl.ds(g * GF, GF)
        rows = pl.ds(g * GC, GC)
        grad = g_ref[:, cols]
        weights = wr_ref[:, rows]
        wide = weights.astype(f32)
        part = wide * dot_nt(grad, bdm_ref[rows, :])
        ds = ((part - wide * sum_slots(part, ones)) * sharp_row(coef_ref, g)).astype(bf16)
        ds_ref[:, rows] = ds
        direct = dot_tn(weights, grad)
        scored = dot_tn(ds, qh_ref[:, cols])
        for i in range(4):
            at = pl.ds(g * GF + i * HEAD, HEAD)
            own = pl.ds(g * GC + i * MEM, MEM)
            mh = bdmh_ref[own, i * HEAD : (i + 1) * HEAD].astype(f32)
            a = scored[i * MEM : (i + 1) * MEM, i * HEAD : (i + 1) * HEAD]
            b = direct[i * MEM : (i + 1) * MEM, i * HEAD : (i + 1) * HEAD]
            a = a - mh * (jnp.sum(mh * a, axis=-1, keepdims=True) * (1.0 / HEAD))
            rho_ref[:, at] = (b + invm_ref[:, 4 * g + i : 4 * g + i + 1] * a).astype(bf16)
        return carry

    for g in range(GROUPS):
        group(g, 0)


def finish_kernel(
    mu_hbm, coef_ref, g_hbm, n_ref, x_hbm, gain_hbm, ww_ref, ds_ref,
    bdmh_ref, bdph_ref, qh_ref, invq_hbm, rs_hbm, w_hbm,
    hidden_hbm, unused_sum, unused_near,
    w_ref, bdd_ref, dq_ref, dn_ref, g_ref, x_ref, hidden_ref, mu_ref, gain_ref, invq_ref, rs_ref, sems,
):
    fetch_mu = pltpu.make_async_copy(mu_hbm, mu_ref, sems.at[0])
    fetch_w = pltpu.make_async_copy(w_hbm, w_ref, sems.at[1])
    fetch_x = pltpu.make_async_copy(x_hbm, x_ref, sems.at[2])
    fetch_g = pltpu.make_async_copy(g_hbm, g_ref, sems.at[3])
    leave = [
        pltpu.make_async_copy(
            hidden_ref.at[:, pl.ds(c * GF, GF)], hidden_hbm.at[:, pl.ds(c * GF, GF)], sems.at[4 + c]
        )
        for c in range(GROUPS)
    ]
    fetch_gain = pltpu.make_async_copy(gain_hbm, gain_ref, sems.at[4 + GROUPS])
    fetch_invq = pltpu.make_async_copy(invq_hbm, invq_ref, sems.at[5 + GROUPS])
    fetch_rs = pltpu.make_async_copy(rs_hbm, rs_ref, sems.at[6 + GROUPS])
    for copy in (fetch_mu, fetch_invq, fetch_gain, fetch_rs, fetch_x, fetch_g, fetch_w):
        copy.start()
    bdd_ref[...] = jnp.zeros_like(bdd_ref)
    fetch_mu.wait()
    fetch_invq.wait()

    def group(g, carry):
        cols = pl.ds(g * GF, GF)
        rows = pl.ds(g * GC, GC)
        for i in range(4):
            h = 4 * g + i
            at = pl.ds(h * HEAD, HEAD)
            keep = coef_ref[:, KEEP + h : KEEP + h + 1]
            mu = mu_ref[:, at]
            own = pl.ds(g * GC + i * MEM, MEM)
            bdd_ref[own, i * HEAD : (i + 1) * HEAD] = (keep * mu).astype(bf16)
        bdd = bdd_ref[rows, :]
        weights = ww_ref[:, rows]
        wide = weights.astype(f32)
        part = wide * dot_nt(n_ref[:, cols], bdd)
        ds = (part - wide * jnp.sum(part, axis=0, keepdims=True)) * sharp_row(coef_ref, g)
        dn_ref[:, cols] = dot_nn(weights, bdd)
        dqh = dot_nn(ds_ref[:, rows], bdmh_ref[rows, :]) + dot_nn(ds.astype(bf16), bdph_ref[rows, :])
        for i in range(4):
            at = pl.ds(g * GF + i * HEAD, HEAD)
            qh = qh_ref[:, at].astype(f32)
            a = dqh[:, i * HEAD : (i + 1) * HEAD]
            a = a - qh * (jnp.sum(qh * a, axis=-1, keepdims=True) * (1.0 / HEAD))
            dq_ref[:, at] = (invq_ref[:, 4 * g + i : 4 * g + i + 1] * a).astype(bf16)
        return carry

    for g in range(GROUPS):
        group(g, 0)
    fetch_gain.wait()
    fetch_rs.wait()
    fetch_x.wait()
    fetch_g.wait()
    fetch_w.wait()
    rs = rs_ref[:, 0:1]

    def project(c, total):
        cols = pl.ds(c * GF, GF)
        dn = dn_ref[:, cols] + dot_nt(dq_ref[...], w_ref[cols, :])
        y = dn * gain_ref[:, cols].astype(f32)
        dn_ref[:, cols] = y
        return total + jnp.sum(y * x_ref[:, cols].astype(f32), axis=-1, keepdims=True)

    total = jnp.zeros((ROWS, 1), f32)
    for c in range(GROUPS):
        total = project(c, total)
    shift = total * rs * rs * (1.0 / D)

    def close(c, carry):
        cols = pl.ds(c * GF, GF)
        dx = rs * (dn_ref[:, cols] - x_ref[:, cols].astype(f32) * shift)
        hidden_ref[:, cols] = (g_ref[:, cols].astype(f32) + dx).astype(bf16)
        leave[c].start()

    for c in range(GROUPS):
        close(c, 0)
    for copy in leave:
        copy.wait()


def call(kernel, outs, ins, scratch=(), flops=0, moved=0, out=VMEM, aliases={}):
    return pl.pallas_call(
        kernel,
        out_shape=[jax.ShapeDtypeStruct(shape, kind) for shape, kind in outs],
        in_specs=ins,
        out_specs=out if isinstance(out, list) else [out] * len(outs),
        scratch_shapes=list(scratch),
        input_output_aliases=aliases,
        compiler_params=pltpu.CompilerParams(vmem_limit_bytes=44 * 1024 * 1024),
        cost_estimate=pl.CostEstimate(flops=flops, bytes_accessed=moved, transcendentals=0),
    )


def place(section, seg):
    return section * SEGS + seg


def pair_swap(value):
    return lax.ppermute(
        value, AXES, [(place(s, j), place(s, j ^ 1)) for s in range(SECTIONS) for j in range(SEGS)]
    )


def chain_sets(parity):
    return [
        (place(s, 2 * p + i), place(s, 2 * p - 1 - i))
        for s in range(SECTIONS)
        for p in range(1, PAIRS)
        if p % 2 == parity
        for i in range(2)
    ]


def hop_sets(parity):
    return [
        (place(s, j), place(s - 1, j))
        for s in range(1, SECTIONS)
        if s % 2 == parity
        for j in range(SEGS)
    ]


def local(x, memory, weight, gain, probes, sharp, persistence, counts, slope):
    x, memory, weight, probes = x[0], memory[0, 0], weight[0], probes[0]
    decay = persistence[0, 0]
    section = lax.axis_index("section")
    seg = lax.axis_index("seg")
    pair = seg // 2

    n, qh, invq, rs, bdm, bdmh, bdph, invm, wr, ww, start = call(
        prepare_kernel,
        [
            ((ROWS, D), bf16), ((ROWS, D), bf16), ((ROWS, HEAD), f32), ((ROWS, HEAD), f32),
            ((GF, GF), bf16), ((GF, GF), bf16), ((GF, GF), bf16), ((MEM, HEAD), f32),
            ((ROWS, GF), bf16), ((ROWS, GF), bf16), ((ROWS, D), bf16),
        ],
        [VMEM, HBM] + [VMEM] * 4 + [SMEM] * 2,
        [pltpu.VMEM((GF, GF), bf16), pltpu.VMEM((D, D), bf16), pltpu.SemaphoreType.DMA],
        flops=2 * ROWS * D * D, moved=10 << 20,
    )(x, weight, gain, memory, probes, slope, sharp, counts)

    other = pair_swap(decay)
    one = jnp.ones_like(decay)
    none = jnp.zeros_like(decay)
    odd = seg % 2 == 1
    coefs = jnp.concatenate(
        [
            jnp.where(odd, other, one), jnp.where(odd, one, decay), jnp.where(odd, none, one),
            jnp.where(odd, one, other), decay * other, 1.0 - decay,
            jnp.broadcast_to(sharp * (1.0 / HEAD), decay.shape), none,
        ],
        axis=1,
    )

    def read(grad):
        return call(
            read_kernel,
            [((MEM, D), bf16), ((ROWS, GF), bf16)],
            [VMEM] * 7,
            flops=2 * ROWS * GF * D, moved=4 << 20,
        )(grad, wr, bdm, bdmh, qh, invm, coefs)

    def finish(mu, grad, ds):
        return call(
            finish_kernel,
            [((ROWS, D), bf16), ((MEM, D), bf16), ((MEM, D), bf16)],
            [HBM, VMEM, HBM, VMEM, HBM, HBM] + [VMEM] * 5 + [HBM] * 3,
            [
                pltpu.VMEM((D, D), bf16), pltpu.VMEM((GF, GF), bf16), pltpu.VMEM((ROWS, D), bf16),
                pltpu.VMEM((ROWS, D), f32), pltpu.VMEM((ROWS, D), bf16), pltpu.VMEM((ROWS, D), bf16),
                pltpu.VMEM((ROWS, D), bf16), pltpu.VMEM((MEM, D), f32), pltpu.VMEM((1, D), bf16),
                pltpu.VMEM((ROWS, HEAD), f32), pltpu.VMEM((ROWS, HEAD), f32),
                pltpu.SemaphoreType.DMA((7 + GROUPS,)),
            ],
            out=[HBM, ANY, ANY],
            flops=2 * ROWS * D * D, moved=12 << 20,
        )(mu, coefs, grad, n, x, gain, ww, ds, bdmh, bdph, qh, invq, rs, weight)

    def join(step, pair_sum, near, moving, mu, carry=None):
        got = [] if carry is None else [carry]
        count = 4 + len(got)
        return call(
            functools.partial(join_kernel, bool(got)),
            [((MEM, D), bf16), ((MEM, D), f32)],
            [SMEM] + [ANY] * (len(got) + 3) + [HBM] * 2,
            [pltpu.VMEM((MEM, D), bf16)] * 3
            + [
                pltpu.VMEM((MEM, HEAD), f32), pltpu.VMEM((MEM, D), bf16), pltpu.VMEM((MEM, D), f32),
                pltpu.SemaphoreType.DMA((6,)),
            ],
            moved=700 << 10, out=HBM, aliases={count: 0, count + 1: 1},
        )(step, pair_sum, near, coefs, *got, moving, mu)

    def blank(*kinds):
        return call(blank_kernel, kinds, [], out=HBM)()

    def first(grad):
        rho, ds = read(grad)
        near = pair_swap(rho)
        pair_sum = call(combine_kernel, [((MEM, D), bf16)], [VMEM] * 3, moved=400 << 10)(rho, near, coefs)[0]
        return pair_sum, near, ds

    def turn(grad):
        def body(step, held):
            moving, mu, ds, hidden = held
            step_now = jnp.reshape(step, (1,))

            def chain(sets):
                def run():
                    got = (lax.ppermute(moving, AXES, sets),) if sets else ()

                    def finishing():
                        new, *unused = finish(mu, grad, ds)
                        return (*unused, ds, new)

                    pair_sum, near, ds_, hidden_ = lax.cond(
                        step == 0, lambda: first(grad) + (hidden,), finishing
                    )
                    return (*join(step_now, pair_sum, near, moving, mu, *got), ds_, hidden_)
                return run

            sends = step == 1
            chain_to = jnp.where(
                pair == jnp.where(sends, 0, PAIRS - 1), 0, jnp.where((pair % 2 == 1) == sends, 1, 2)
            )
            return tuple(
                lax.switch(chain_to, [chain(None), chain(chain_sets(1)), chain(chain_sets(0))])
            )

        held = blank(((MEM, D), bf16), ((MEM, D), f32), ((ROWS, GF), bf16), ((ROWS, D), bf16))
        held = lax.fori_loop(0, two, body, tuple(held))
        return held[3], held[1]

    def hop(step, held):
        grad, hidden, mu = held
        sends = step == 1
        hop_to = jnp.where(
            section == jnp.where(sends, 0, SECTIONS - 1), 0, jnp.where((section % 2 == 1) == sends, 1, 2)
        )
        grad = lax.switch(
            hop_to,
            [
                lambda: grad,
                lambda: lax.ppermute(hidden, AXES, hop_sets(1)),
                lambda: lax.ppermute(hidden, AXES, hop_sets(0)),
            ],
        )
        hidden, mu = lax.cond(sends, lambda: (hidden, mu), lambda: tuple(turn(grad)))
        return grad, hidden, mu

    two = jnp.minimum(counts[0], 2)
    state = lax.fori_loop(
        0, two, hop, (start, *blank(((ROWS, D), bf16), ((MEM, D), f32)))
    )[1:]
    return state[0][None], state[1][None, None]


def solution(mesh):
    placed = (
        P("section", "seg", None),
        P("section", "seg", None, None),
        P("section", None, None),
        P("section", None),
        P("section", None, None),
        P("section", None),
        P("section", "seg", None, None),
        P("seg"),
        P("seg", None),
    )
    return jax.shard_map(
        local,
        mesh=mesh,
        in_specs=placed,
        out_specs=(P("section", "seg", None), P("section", "seg", None, None)),
        check_vma=False,
    )
```

time: 518 us -> 401 us (0.77); the launches traced: 512 us -> 401 us
  waiting for transfers between devices: 446 us -> 367 us
  starting transfers between devices: 17.3 us -> 2.58 us
  loops' own time: 8.8 us -> 0.76 us
  other arithmetic: 7.51 us -> 0.67 us
    ppermute x12 -> x4, waiting for transfers between devices: 446 us -> 367 us  [the longest x1 356 us: hop(): lax.ppermute(hidden, AXES, hop_sets(1))]
    ppermute x12 -> x4, starting transfers between devices: 17.3 us -> 2.58 us  [the longest x1 1.29 us: hop(): lax.ppermute(hidden, AXES, hop_sets(1))]
    another operation x15 -> x10, loops' own time: 8.8 us -> 0.76 us  [the longest x1 0.51 us: local(): lax.fori_loop(0, two, hop, (start, *blank(((ROWS, D), bf16), ((MEM, D), f...]
    pallas_call x2 -> x7, Pallas kernels: 13.6 us -> 15.8 us  [the longest x1 8.78 us: finish(): call(finish_kernel, [((ROWS, D), bf16), ((MEM, D), bf16), ((MEM, D), bf16...]
  transfers between devices with their start and end apart: 12 -> 4, of which waited for: 5 -> 3; matrix products, arithmetic and copies ran while one was open for 1% -> 0% of each run, Pallas kernels for 2% -> 3%
where the time goes in v2:
time: 401 us
  waiting for transfers between devices  367 us (92%)
  Pallas kernels  24.1 us (6%)
  local copies, waits for them, and re-layouts  4.38 us (1%)
    ppermute x1, waiting for transfers between devices, hop(): lax.ppermute(hidden, AXES, hop_sets(1))  356 us
    pallas_call x1, Pallas kernels, finish(): call(finish_kernel, [((ROWS, D), bf16), ((MEM, D), bf16), ((MEM, D), bf16...  8.78 us
    pallas_call x1, Pallas kernels, local(): call(prepare_kernel, [((ROWS, D), bf16), ((ROWS, D), bf16), ((ROWS, HEAD)...  8.26 us
  transfers between devices with their start and end apart: 4, of which 3 were waited for; matrix products, arithmetic and copies ran while one was open for 0% of the time, Pallas kernels for 3%

profile of v2, /device:TPU:0, one launch (start us, length us, event | category | flops | bytes accessed | tf_op | source)
XLA Modules:
  0.0 401.0 jit_solution(1642603519745587080)
XLA Ops:
  0.6 0.8 copy.17
  1.4 0.0 collective-permute-start.7
  1.4 0.7 multiply_bitcast_fusion
  2.7 0.0 copy-start
  2.7 1.0 copy-done
  3.8 0.0 copy-start.1
  3.8 0.9 copy-done.1
  4.7 0.0 copy-start.2
  4.7 0.9 copy-done.2
  5.6 0.0 copy-start.3
  5.6 0.7 copy-done.3
  6.2 0.0 copy-start.4
  6.2 8.3 %shard_map.104 = (bf16[128,2048]{1,0:T(8,128)(2,1)S(1)}, bf16[128,2048]{1,0:T(8,128)(2,1)S(1)}, f32[128,128]{1,0:T(8,128)}, f32[128,128]{1,0:T(8,128)}, bf16[512...) custom-call(bf16[128,2048]{1,0:T(8,128)(2,1)} %bitcast.20, ...), custom_call_target="tpu_custom_call" | custom-call | flops 1073741824 | bytes 10485760 | tf_op jit(solution)/shard_map/pallas_call | solution.py:352
  14.6 0.0 collective-permute-done.7
  14.6 0.1 concatenate.3
  14.7 0.0 copy-done.4
  14.7 386.0 %while.43 = (s32[]{:T(128)}, bf16[128,2048]{1,0:T(8,128)(2,1)}, bf16[128,2048]{1,0:T(8,128)(2,1)}, f32[32,2048]{1,0:T(8,128)}, s32[]{:T(128)}, /*index=5*/s32[]{...) while((s32[]{:T(128)}, bf16[128,2048]{1,0:T(8,128)(2,1)}, ...), condition=%wide.region_17.18_spmd, body=%wide.region_0.17_spmd.sunk | while | flops 1073741824 | bytes 15922971 | solution.py:474
  15.0 357.4 %conditional.9 = (bf16[128,2048]{1,0:T(8,128)(2,1)}) conditional(s32[]{:T(128)} %clamp.12, bf16[128,2048]{1,0:T(8,128)(2,1)} %get-tuple-element.1576, bf16[128,2048]{1,0:T(8,128)(2,1)} %get-tuple-element.1577, bf16[128,2048]{1,0:T(8,128)(2,1)} %get-tuple-element.1577), branch_computations={%region_1.1_spmd, %region_2.2_spmd, %region_3.3_spmd} | conditional | bytes 2097200 | solution.py:462
  15.0 1.3 collective-permute-start
  16.3 356.1 %collective-permute-done = bf16[128,2048]{1,0:T(8,128)(2,1)} collective-permute-done((bf16[128,2048]{1,0:T(8,128)(2,1)}, bf16[128,2048]{1,0:T(8,128)(2,1)}, u32[]{:S(2)}, u32[]{:S(2)}) %collective-permute-start) | collective-permute-done | bytes 524320 | tf_op jit(solution)/shard_map/while/body/cond/branch_1_fun/ppermute | solution.py:466
  372.4 28.1 %conditional.10 = ((bf16[128,2048]{1,0:T(8,128)(2,1)}, f32[32,2048]{1,0:T(8,128)})) conditional(s32[]{:T(128)} %convert_element_type.15, (s32[]{:T(128)}, s32[]{:T(128)}, f32[32,128]{1,0:T(8,128)S(1)}, bf16[128,2048]{1,0:T(8,128)(2,1)}, bf16[128,2048]{1,0:T(8,128)(2,1)S(1)}, /*index=5*/bf16[128,2048]{1,0:T(8,128)(2,1)S(1)}, ...), branch_computations={%region_4.15_spmd, %region_16.16_spmd} | conditional | flops 1073741824 | bytes 13825309 | solution.py:470
  372.4 28.1 %while.42 = (s32[]{:T(128)}, bf16[32,2048]{1,0:T(8,128)(2,1)S(1)}, f32[32,2048]{1,0:T(8,128)}, bf16[128,512]{1,0:T(8,128)(2,1)}, bf16[128,2048]{1,0:T(8,128)(2,1...) while((s32[]{:T(128)}, bf16[32,2048]{1,0:T(8,128)(2,1)S(1)}, ...), condition=%wide.region_15.14_spmd, body=%wide.region_5.13_spmd.sunk | while | flops 1073741824 | bytes 13824943 | solution.py:453
  372.4 19.1 %conditional.11 = (bf16[32,2048]{1,0:T(8,128)(2,1)S(1)}, f32[32,2048]{1,0:T(8,128)}, bf16[128,512]{1,0:T(8,128)(2,1)}, bf16[128,2048]{1,0:T(8,128)(2,1)}) conditional(s32[]{:T(128)} %clamp.13, (s32[]{:T(128)}, f32[32,2048]{1,0:T(8,128)}, f32[32,128]{1,0:T(8,128)S(1)}, bf16[128,2048]{1,0:T(8,128)(2,1)}, ...), branch_computations={%region_6.6_spmd, %region_9.9_spmd, %region_12.12_spmd} | conditional | flops 1073741824 | bytes 13824294 | solution.py:449
  372.4 1.3 collective-permute-start.4
  373.7 9.8 %conditional.1 = (bf16[32,2048]{1,0:T(8,128)(2,1)S(1)}, bf16[32,2048]{1,0:T(8,128)(2,1)}, bf16[128,512]{1,0:T(8,128)(2,1)}, bf16[128,2048]{1,0:T(8,128)(2,1)}) conditional(s32[]{:T(128)} %convert_element_type.11, (f32[32,2048]{1,0:T(8,128)}, f32[32,128]{1,0:T(8,128)S(1)}, bf16[128,2048]{1,0:T(8,128)(2,1)}, bf16[128,2048]{1,0:T(8,128)(2,1)S(1)}, ...), branch_computations={%region_10.7_spmd, %region_11.8_spmd} | conditional | flops 1073741824 | bytes 12582944 | solution.py:438
  373.7 3.6 branch_1_fun.9
  377.2 0.0 collective-permute-start.3
  377.2 5.1 %collective-permute-done.3.get_ref = bf16[32,2048]{1,0:T(8,128)(2,1)} collective-permute-done((bf16[32,2048]{1,0:T(8,128)(2,1)S(1)}, bf16[32,2048]{1,0:T(8,128)(2,1)}, u32[]{:S(2)}, u32[]{:S(2)}) %collective-permute-start.3) | collective-permute-done | bytes 131104 | tf_op jit(solution)/shard_map/while/body/cond/branch_0_fun/while/body/cond/branch_1_fun/cond/branch_1_fun/ppermute | solution.py:321
  382.3 1.2 branch_1_fun.10
  383.5 5.8 %collective-permute-done.4.refs_0_ = bf16[32,2048]{1,0:T(8,128)(2,1)S(1)} collective-permute-done((bf16[32,2048]{1,0:T(8,128)(2,1)S(1)}, bf16[32,2048]{1,0:T(8,128)(2,1)S(1)}, u32[]{:S(2)}, u32[]{:S(2)}) %collective-permute-start.4) | collective-permute-done | bytes 131104 | tf_op jit(solution)/shard_map/while/body/cond/branch_0_fun/while/body/cond/branch_1_fun/ppermute | solution.py:432
  389.2 2.2 branch_1_fun.11
  391.5 8.9 %conditional.11 = (bf16[32,2048]{1,0:T(8,128)(2,1)S(1)}, f32[32,2048]{1,0:T(8,128)}, bf16[128,512]{1,0:T(8,128)(2,1)}, bf16[128,2048]{1,0:T(8,128)(2,1)}) conditional(s32[]{:T(128)} %clamp.13, (s32[]{:T(128)}, f32[32,2048]{1,0:T(8,128)}, f32[32,128]{1,0:T(8,128)S(1)}, bf16[128,2048]{1,0:T(8,128)(2,1)}, ...), branch_computations={%region_6.6_spmd, %region_9.9_spmd, %region_12.12_spmd} | conditional | flops 1073741824 | bytes 13824294 | solution.py:449
  391.5 8.8 %conditional = (bf16[32,2048]{1,0:T(8,128)(2,1)S(1)}, bf16[32,2048]{1,0:T(8,128)(2,1)}, bf16[128,512]{1,0:T(8,128)(2,1)}, bf16[128,2048]{1,0:T(8,128)(2,1)}) conditional(s32[]{:T(128)} %convert_element_type.10, (f32[32,2048]{1,0:T(8,128)}, f32[32,128]{1,0:T(8,128)S(1)}, bf16[128,2048]{1,0:T(8,128)(2,1)}, bf16[128,2048]{1,0:T(8,128)(2,1)S(1)}, ...), branch_computations={%region_7.4_spmd, %region_8.5_spmd} | conditional | flops 1073741824 | bytes 12582944 | solution.py:438
  391.6 8.8 %branch_0_fun.5 = (bf16[128,2048]{1,0:T(8,128)(2,1)}, bf16[32,2048]{1,0:T(8,128)(2,1)S(1)}, bf16[32,2048]{1,0:T(8,128)(2,1)}) custom-call(f32[32,2048]{1,0:T(8,128)} %get-tuple-element.775.mu_hbm, f32[32,128]{1,0:T(8,128)S(1)} %get-tuple-element.776.coef_ref, bf16[128,2048]{1,0:T(8,128)(2,1)} %get-tuple-element.777.g_hbm, ...), custom_call_target="tpu_custom_call" | custom-call | flops 1073741824 | bytes 12582912 | tf_op jit(solution)/shard_map/while/body/cond/branch_0_fun/while/body/cond/branch_0_fun/cond/branch_0_fun/pallas_call | solution.py:386
  400.4 0.1 branch_0_fun.6
  (8 shorter events, 0.0 us)
Async XLA Ops:
  1.4 13.2 %collective-permute-start.7 = (f32[32,16]{1,0:T(8,128)S(1)}, f32[32,16]{1,0:T(8,128)S(1)}, u32[]{:S(2)}, u32[]{:S(2)}) collective-permute-start(f32[32,16]{1,0:T(8,128)S(1)} %bitcast.22), channel_id=1, source_target_pairs={{0,1},{1,0},{2,3},{3,2},{4,5},{5,4},{6,7},{7,6},{8,9},{9,8},{10,11... | collective-permute-start | bytes 6152 | tf_op jit(solution)/shard_map/ppermute | solution.py:321
  2.7 1.0 copy-start
  3.8 0.9 copy-start.1
  4.7 0.9 copy-start.2
  5.6 0.7 copy-start.3
  6.2 8.5 %copy-start.4 = (bf16[1,128,2048]{2,1,0:T(8,128)(2,1)S(1)}, bf16[1,128,2048]{2,1,0:T(8,128)(2,1)}, u32[]{:S(2)}) copy-start(bf16[1,128,2048]{2,1,0:T(8,128)(2,1)} %param.27) | copy-start | bytes 1572868
  15.0 357.4 %collective-permute-start = (bf16[128,2048]{1,0:T(8,128)(2,1)}, bf16[128,2048]{1,0:T(8,128)(2,1)}, u32[]{:S(2)}, u32[]{:S(2)}) collective-permute-start(bf16[128,2048]{1,0:T(8,128)(2,1)} %param.1), channel_id=1, source_target_pairs={{32,0},{33,1},{34,2},{35,3},{36,4},{37,5},{38,6},{39,7},{40,8},{41... | collective-permute-start | bytes 1572872 | tf_op jit(solution)/shard_map/while/body/cond/branch_1_fun/ppermute | solution.py:466
  372.4 16.9 %collective-permute-start.4 = (bf16[32,2048]{1,0:T(8,128)(2,1)S(1)}, bf16[32,2048]{1,0:T(8,128)(2,1)S(1)}, u32[]{:S(2)}, u32[]{:S(2)}) collective-permute-start(bf16[32,2048]{1,0:T(8,128)(2,1)S(1)} %get-tuple-element.878.refs_1_), channel_id=1, source_target_pairs={{2,1},{3,0},{6,5},{7,4},{10,9},{11,8},{14,13},{15,12},{18,17},{19,... | collective-permute-start | bytes 393224 | tf_op jit(solution)/shard_map/while/body/cond/branch_0_fun/while/body/cond/branch_1_fun/ppermute | solution.py:432
  377.2 5.1 %collective-permute-start.3 = (bf16[32,2048]{1,0:T(8,128)(2,1)S(1)}, bf16[32,2048]{1,0:T(8,128)(2,1)}, u32[]{:S(2)}, u32[]{:S(2)}) collective-permute-start(bf16[32,2048]{1,0:T(8,128)(2,1)S(1)} %get-tuple-element.853.rho_ref), channel_id=1, source_target_pairs={{0,1},{1,0},{2,3},{3,2},{4,5},{5,4},{6,7},{7,6},{8,9},{9,8},{10,11... | collective-permute-start | bytes 393224 | tf_op jit(solution)/shard_map/while/body/cond/branch_0_fun/while/body/cond/branch_1_fun/cond/branch_1_fun/ppermute | solution.py:321

commit v3 on v2

--- a/solution.py
+++ b/solution.py
@@ -157,8 +157,15 @@
         if has_carry:
             sources.append((carry_any, carry_ref))
         fetch = [pltpu.make_async_copy(*pair, sems.at[k]) for k, pair in enumerate(sources)]
-        leave_moving = pltpu.make_async_copy(moving_ref, moving_hbm, sems.at[4])
-        leave_mu = pltpu.make_async_copy(mu_ref, mu_hbm, sems.at[5])
+        halves = [pl.ds(k * (D // 2), D // 2) for k in range(2)]
+        leave_moving = [
+            pltpu.make_async_copy(moving_ref.at[:, half], moving_hbm.at[:, half], sems.at[4 + k])
+            for k, half in enumerate(halves)
+        ]
+        leave_mu = [
+            pltpu.make_async_copy(mu_ref.at[:, half], mu_hbm.at[:, half], sems.at[6 + k])
+            for k, half in enumerate(halves)
+        ]
         for copy in fetch:
             copy.start()
         for copy in fetch:
@@ -175,10 +182,11 @@
                 mu = mu + reach * carry
             moving_ref[:, at] = moving
             mu_ref[:, at] = mu
-        leave_moving.start()
-        leave_mu.start()
-        leave_moving.wait()
-        leave_mu.wait()
+            if (h + 1) % (HEADS // 2) == 0:
+                leave_mu[h // (HEADS // 2)].start()
+                leave_moving[h // (HEADS // 2)].start()
+        for copy in leave_moving + leave_mu:
+            copy.wait()
 
 
 def combine_kernel(rho_ref, get_ref, coef_ref, out_ref):
@@ -199,7 +207,7 @@
         weights = wr_ref[:, rows]
         wide = weights.astype(f32)
         part = wide * dot_nt(grad, bdm_ref[rows, :])
-        ds = ((part - wide * sum_slots(part, ones)) * sharp_row(coef_ref, g)).astype(bf16)
+        ds = ((part - wide * dot_nn(part.astype(bf16), ones)) * sharp_row(coef_ref, g)).astype(bf16)
         ds_ref[:, rows] = ds
         direct = dot_tn(weights, grad)
         scored = dot_tn(ds, qh_ref[:, cols])
@@ -236,7 +244,7 @@
     fetch_gain = pltpu.make_async_copy(gain_hbm, gain_ref, sems.at[4 + GROUPS])
     fetch_invq = pltpu.make_async_copy(invq_hbm, invq_ref, sems.at[5 + GROUPS])
     fetch_rs = pltpu.make_async_copy(rs_hbm, rs_ref, sems.at[6 + GROUPS])
-    for copy in (fetch_mu, fetch_invq, fetch_gain, fetch_rs, fetch_x, fetch_g, fetch_w):
+    for copy in (fetch_mu, fetch_invq, fetch_w, fetch_gain, fetch_rs, fetch_x, fetch_g):
         copy.start()
     bdd_ref[...] = jnp.zeros_like(bdd_ref)
     fetch_mu.wait()
@@ -408,7 +416,7 @@
             [pltpu.VMEM((MEM, D), bf16)] * 3
             + [
                 pltpu.VMEM((MEM, HEAD), f32), pltpu.VMEM((MEM, D), bf16), pltpu.VMEM((MEM, D), f32),
-                pltpu.SemaphoreType.DMA((6,)),
+                pltpu.SemaphoreType.DMA((8,)),
             ],
             moved=700 << 10, out=HBM, aliases={count: 0, count + 1: 1},
         )(step, pair_sum, near, coefs, *got, moving, mu)

time: 401 us -> 398 us (level)
  no operation moved by 1% of the time
where the time goes in v3:
time: 398 us; the launch traced here: 397 us
  waiting for transfers between devices  364 us (91%)
  Pallas kernels  23.7 us (6%)
  local copies, waits for them, and re-layouts  4.38 us (1%)
    ppermute x1, waiting for transfers between devices, hop(): lax.ppermute(hidden, AXES, hop_sets(1))  353 us
    pallas_call x1, Pallas kernels, finish(): call(finish_kernel, [((ROWS, D), bf16), ((MEM, D), bf16), ((MEM, D), bf16...  8.63 us
    pallas_call x1, Pallas kernels, local(): call(prepare_kernel, [((ROWS, D), bf16), ((ROWS, D), bf16), ((ROWS, HEAD)...  8.26 us
  transfers between devices with their start and end apart: 4, of which 3 were waited for; matrix products, arithmetic and copies ran while one was open for 0% of the time, Pallas kernels for 3%

profile of v3, /device:TPU:0, one launch (start us, length us, event | category | flops | bytes accessed | tf_op | source)
XLA Modules:
  0.0 397.4 jit_solution(13989915705703176042)
XLA Ops:
  0.6 0.8 copy.17
  1.4 0.0 collective-permute-start.7
  1.4 0.7 multiply_bitcast_fusion
  2.7 0.0 copy-start
  2.7 1.0 copy-done
  3.8 0.0 copy-start.1
  3.8 0.9 copy-done.1
  4.7 0.0 copy-start.2
  4.7 0.9 copy-done.2
  5.6 0.0 copy-start.3
  5.6 0.7 copy-done.3
  6.2 0.0 copy-start.4
  6.2 8.3 %shard_map.104 = (bf16[128,2048]{1,0:T(8,128)(2,1)S(1)}, bf16[128,2048]{1,0:T(8,128)(2,1)S(1)}, f32[128,128]{1,0:T(8,128)}, f32[128,128]{1,0:T(8,128)}, bf16[512...) custom-call(bf16[128,2048]{1,0:T(8,128)(2,1)} %bitcast.20, ...), custom_call_target="tpu_custom_call" | custom-call | flops 1073741824 | bytes 10485760 | tf_op jit(solution)/shard_map/pallas_call | solution.py:360
  14.6 0.0 collective-permute-done.7
  14.6 0.1 concatenate.3
  14.7 0.0 copy-done.4
  14.7 382.4 %while.43 = (s32[]{:T(128)}, bf16[128,2048]{1,0:T(8,128)(2,1)}, bf16[128,2048]{1,0:T(8,128)(2,1)}, f32[32,2048]{1,0:T(8,128)}, s32[]{:T(128)}, /*index=5*/s32[]{...) while((s32[]{:T(128)}, bf16[128,2048]{1,0:T(8,128)(2,1)}, ...), condition=%wide.region_17.18_spmd, body=%wide.region_0.17_spmd.sunk | while | flops 1073741824 | bytes 15922971 | solution.py:482
  15.0 354.0 %conditional.9 = (bf16[128,2048]{1,0:T(8,128)(2,1)}) conditional(s32[]{:T(128)} %clamp.12, bf16[128,2048]{1,0:T(8,128)(2,1)} %get-tuple-element.1576, bf16[128,2048]{1,0:T(8,128)(2,1)} %get-tuple-element.1577, bf16[128,2048]{1,0:T(8,128)(2,1)} %get-tuple-element.1577), branch_computations={%region_1.1_spmd, %region_2.2_spmd, %region_3.3_spmd} | conditional | bytes 2097200 | solution.py:470
  15.0 1.3 collective-permute-start
  16.3 352.7 %collective-permute-done = bf16[128,2048]{1,0:T(8,128)(2,1)} collective-permute-done((bf16[128,2048]{1,0:T(8,128)(2,1)}, bf16[128,2048]{1,0:T(8,128)(2,1)}, u32[]{:S(2)}, u32[]{:S(2)}) %collective-permute-start) | collective-permute-done | bytes 524320 | tf_op jit(solution)/shard_map/while/body/cond/branch_1_fun/ppermute | solution.py:474
  369.0 27.9 %conditional.10 = ((bf16[128,2048]{1,0:T(8,128)(2,1)}, f32[32,2048]{1,0:T(8,128)})) conditional(s32[]{:T(128)} %convert_element_type.15, (s32[]{:T(128)}, s32[]{:T(128)}, f32[32,128]{1,0:T(8,128)S(1)}, bf16[128,2048]{1,0:T(8,128)(2,1)}, bf16[128,2048]{1,0:T(8,128)(2,1)S(1)}, /*index=5*/bf16[128,2048]{1,0:T(8,128)(2,1)S(1)}, ...), branch_computations={%region_4.15_spmd, %region_16.16_spmd} | conditional | flops 1073741824 | bytes 13825309 | solution.py:478
  369.0 27.9 %while.42 = (s32[]{:T(128)}, bf16[32,2048]{1,0:T(8,128)(2,1)S(1)}, f32[32,2048]{1,0:T(8,128)}, bf16[128,512]{1,0:T(8,128)(2,1)}, bf16[128,2048]{1,0:T(8,128)(2,1...) while((s32[]{:T(128)}, bf16[32,2048]{1,0:T(8,128)(2,1)S(1)}, ...), condition=%wide.region_15.14_spmd, body=%wide.region_5.13_spmd.sunk | while | flops 1073741824 | bytes 13824943 | solution.py:461
  369.0 19.0 %conditional.11 = (bf16[32,2048]{1,0:T(8,128)(2,1)S(1)}, f32[32,2048]{1,0:T(8,128)}, bf16[128,512]{1,0:T(8,128)(2,1)}, bf16[128,2048]{1,0:T(8,128)(2,1)}) conditional(s32[]{:T(128)} %clamp.13, (s32[]{:T(128)}, f32[32,2048]{1,0:T(8,128)}, f32[32,128]{1,0:T(8,128)S(1)}, bf16[128,2048]{1,0:T(8,128)(2,1)}, ...), branch_computations={%region_6.6_spmd, %region_9.9_spmd, %region_12.12_spmd} | conditional | flops 1073741824 | bytes 13824294 | solution.py:457
  369.0 1.3 collective-permute-start.4
  370.3 9.7 %conditional.1 = (bf16[32,2048]{1,0:T(8,128)(2,1)S(1)}, bf16[32,2048]{1,0:T(8,128)(2,1)}, bf16[128,512]{1,0:T(8,128)(2,1)}, bf16[128,2048]{1,0:T(8,128)(2,1)}) conditional(s32[]{:T(128)} %convert_element_type.11, (f32[32,2048]{1,0:T(8,128)}, f32[32,128]{1,0:T(8,128)S(1)}, bf16[128,2048]{1,0:T(8,128)(2,1)}, bf16[128,2048]{1,0:T(8,128)(2,1)S(1)}, ...), branch_computations={%region_10.7_spmd, %region_11.8_spmd} | conditional | flops 1073741824 | bytes 12582944 | solution.py:446
  370.3 3.5 branch_1_fun.9
  373.8 0.0 collective-permute-start.3
  373.8 5.1 %collective-permute-done.3.get_ref = bf16[32,2048]{1,0:T(8,128)(2,1)} collective-permute-done((bf16[32,2048]{1,0:T(8,128)(2,1)S(1)}, bf16[32,2048]{1,0:T(8,128)(2,1)}, u32[]{:S(2)}, u32[]{:S(2)}) %collective-permute-start.3) | collective-permute-done | bytes 131104 | tf_op jit(solution)/shard_map/while/body/cond/branch_0_fun/while/body/cond/branch_1_fun/cond/branch_1_fun/ppermute | solution.py:329
  378.8 1.2 branch_1_fun.10
  380.0 5.9 %collective-permute-done.4.refs_0_ = bf16[32,2048]{1,0:T(8,128)(2,1)S(1)} collective-permute-done((bf16[32,2048]{1,0:T(8,128)(2,1)S(1)}, bf16[32,2048]{1,0:T(8,128)(2,1)S(1)}, u32[]{:S(2)}, u32[]{:S(2)}) %collective-permute-start.4) | collective-permute-done | bytes 131104 | tf_op jit(solution)/shard_map/while/body/cond/branch_0_fun/while/body/cond/branch_1_fun/ppermute | solution.py:440
  385.9 2.1 branch_1_fun.11
  388.1 8.8 %conditional.11 = (bf16[32,2048]{1,0:T(8,128)(2,1)S(1)}, f32[32,2048]{1,0:T(8,128)}, bf16[128,512]{1,0:T(8,128)(2,1)}, bf16[128,2048]{1,0:T(8,128)(2,1)}) conditional(s32[]{:T(128)} %clamp.13, (s32[]{:T(128)}, f32[32,2048]{1,0:T(8,128)}, f32[32,128]{1,0:T(8,128)S(1)}, bf16[128,2048]{1,0:T(8,128)(2,1)}, ...), branch_computations={%region_6.6_spmd, %region_9.9_spmd, %region_12.12_spmd} | conditional | flops 1073741824 | bytes 13824294 | solution.py:457
  388.1 8.7 %conditional = (bf16[32,2048]{1,0:T(8,128)(2,1)S(1)}, bf16[32,2048]{1,0:T(8,128)(2,1)}, bf16[128,512]{1,0:T(8,128)(2,1)}, bf16[128,2048]{1,0:T(8,128)(2,1)}) conditional(s32[]{:T(128)} %convert_element_type.10, (f32[32,2048]{1,0:T(8,128)}, f32[32,128]{1,0:T(8,128)S(1)}, bf16[128,2048]{1,0:T(8,128)(2,1)}, bf16[128,2048]{1,0:T(8,128)(2,1)S(1)}, ...), branch_computations={%region_7.4_spmd, %region_8.5_spmd} | conditional | flops 1073741824 | bytes 12582944 | solution.py:446
  388.1 8.6 %branch_0_fun.5 = (bf16[128,2048]{1,0:T(8,128)(2,1)}, bf16[32,2048]{1,0:T(8,128)(2,1)S(1)}, bf16[32,2048]{1,0:T(8,128)(2,1)}) custom-call(f32[32,2048]{1,0:T(8,128)} %get-tuple-element.775.mu_hbm, f32[32,128]{1,0:T(8,128)S(1)} %get-tuple-element.776.coef_ref, bf16[128,2048]{1,0:T(8,128)(2,1)} %get-tuple-element.777.g_hbm, ...), custom_call_target="tpu_custom_call" | custom-call | flops 1073741824 | bytes 12582912 | tf_op jit(solution)/shard_map/while/body/cond/branch_0_fun/while/body/cond/branch_0_fun/cond/branch_0_fun/pallas_call | solution.py:394
  396.7 0.1 branch_0_fun.6
  (8 shorter events, 0.0 us)
Async XLA Ops:
  1.4 13.2 %collective-permute-start.7 = (f32[32,16]{1,0:T(8,128)S(1)}, f32[32,16]{1,0:T(8,128)S(1)}, u32[]{:S(2)}, u32[]{:S(2)}) collective-permute-start(f32[32,16]{1,0:T(8,128)S(1)} %bitcast.22), channel_id=1, source_target_pairs={{0,1},{1,0},{2,3},{3,2},{4,5},{5,4},{6,7},{7,6},{8,9},{9,8},{10,11... | collective-permute-start | bytes 6152 | tf_op jit(solution)/shard_map/ppermute | solution.py:329
  2.7 1.0 copy-start
  3.8 0.9 copy-start.1
  4.7 0.9 copy-start.2
  5.6 0.7 copy-start.3
  6.2 8.5 %copy-start.4 = (bf16[1,128,2048]{2,1,0:T(8,128)(2,1)S(1)}, bf16[1,128,2048]{2,1,0:T(8,128)(2,1)}, u32[]{:S(2)}) copy-start(bf16[1,128,2048]{2,1,0:T(8,128)(2,1)} %param.27) | copy-start | bytes 1572868
  15.0 354.0 %collective-permute-start = (bf16[128,2048]{1,0:T(8,128)(2,1)}, bf16[128,2048]{1,0:T(8,128)(2,1)}, u32[]{:S(2)}, u32[]{:S(2)}) collective-permute-start(bf16[128,2048]{1,0:T(8,128)(2,1)} %param.1), channel_id=1, source_target_pairs={{32,0},{33,1},{34,2},{35,3},{36,4},{37,5},{38,6},{39,7},{40,8},{41... | collective-permute-start | bytes 1572872 | tf_op jit(solution)/shard_map/while/body/cond/branch_1_fun/ppermute | solution.py:474
  369.0 16.9 %collective-permute-start.4 = (bf16[32,2048]{1,0:T(8,128)(2,1)S(1)}, bf16[32,2048]{1,0:T(8,128)(2,1)S(1)}, u32[]{:S(2)}, u32[]{:S(2)}) collective-permute-start(bf16[32,2048]{1,0:T(8,128)(2,1)S(1)} %get-tuple-element.878.refs_1_), channel_id=1, source_target_pairs={{2,1},{3,0},{6,5},{7,4},{10,9},{11,8},{14,13},{15,12},{18,17},{19,... | collective-permute-start | bytes 393224 | tf_op jit(solution)/shard_map/while/body/cond/branch_0_fun/while/body/cond/branch_1_fun/ppermute | solution.py:440
  373.8 5.1 %collective-permute-start.3 = (bf16[32,2048]{1,0:T(8,128)(2,1)S(1)}, bf16[32,2048]{1,0:T(8,128)(2,1)}, u32[]{:S(2)}, u32[]{:S(2)}) collective-permute-start(bf16[32,2048]{1,0:T(8,128)(2,1)S(1)} %get-tuple-element.853.rho_ref), channel_id=1, source_target_pairs={{0,1},{1,0},{2,3},{3,2},{4,5},{5,4},{6,7},{7,6},{8,9},{9,8},{10,11... | collective-permute-start | bytes 393224 | tf_op jit(solution)/shard_map/while/body/cond/branch_0_fun/while/body/cond/branch_1_fun/cond/branch_1_fun/ppermute | solution.py:329
